TPU v7x, 128 devices: a whole 4x4x4 slice. The times are simulated.
128 devices in a mesh: dp: 16 (over y_hi, z, core), head: 8 (over y_lo, x).
Axes of the slice: x: 4, y: 4 (y_hi: 2, y_lo: 2; y = y_hi * 2 + y_lo), z: 4, core: 2. Of those that a mesh axis runs over, the one named last changes fastest.
Arguments:
- projections: bfloat16 [3, 16384, 3072], P(None, ('dp', 'head')), may hold values from -16 to 16
- projection_tangent: bfloat16 [3, 16384, 3072], P(None, ('dp', 'head')), may hold values from -6 to 6
- position_ids: int32 [16384, 3], P(('dp', 'head')), may hold values from 0 to 63
- norm_gain: float32 [2, 3072], replicated, may hold values from 0.5 to 1.5
- out_weight: bfloat16 [3072, 5120], P('dp', 'head'), may hold values from -0.109375 to 0.109375
- timestep: int32 [16], replicated, may hold values from 0 to 999
- time_tangent: float32 [16], replicated, may hold values from 0.5 to 2
- gate_weight: bfloat16 [256, 5120], P('dp'), may hold values from -0.375 to 0.375
- residual: bfloat16 [16384, 5120], P('dp', 'head'), may hold values from -6 to 6
- residual_tangent: bfloat16 [16384, 5120], P('dp', 'head'), may hold values from -6 to 6
Outputs:
- block_out: bfloat16 [16384, 5120], P('dp', 'head')
- block_tangent: bfloat16 [16384, 5120], P('dp', 'head')
All inputs are finite; a program needn't handle non-finite values.
Results may differ from a plain program's by a relative error of at most 0.0085.
Values may be sent and summed in bfloat16 or wider, within the bound.
A program may use at most 128 MiB of HBM per device.

v0:
```python
import jax
import jax.numpy as jnp
import numpy as np
from jax import lax
from jax.sharding import PartitionSpec as P

HEAD_DIM = 128
FREQ = 256


EPSILON = 1e-06


def rope_angles(position_ids):
    pair_count = HEAD_DIM // 2
    height_pairs = HEAD_DIM // 6
    time_pairs = pair_count - 2 * height_pairs
    pair_index = np.arange(pair_count)
    axis_pick = np.where(
        pair_index < time_pairs, 0, np.where(pair_index < time_pairs + height_pairs, 1, 2)
    )
    local_idx = np.where(
        axis_pick == 0,
        pair_index,
        np.where(axis_pick == 1, pair_index - time_pairs, pair_index - time_pairs - height_pairs),
    )
    span_count = np.where(axis_pick == 0, time_pairs, height_pairs)
    frequency = np.power(10000.0, -local_idx / span_count).astype(np.float32)
    chosen = position_ids.astype(jnp.float32)[:, axis_pick]
    angles = jnp.repeat(chosen * jnp.asarray(frequency), 2, axis=1)
    return (jnp.cos(angles), jnp.sin(angles))


def rotate(matrix, cosine, sine_part):
    row_count = matrix.shape[0]
    heads_here = matrix.shape[1] // HEAD_DIM
    pairs_view = matrix.reshape(row_count, heads_here, HEAD_DIM // 2, 2)
    swapped = jnp.stack([-pairs_view[..., 1], pairs_view[..., 0]], axis=-1).reshape(
        row_count, heads_here, HEAD_DIM
    )
    grouped = matrix.reshape(row_count, heads_here, HEAD_DIM)
    turned = grouped * cosine[:, None, :] + swapped * sine_part[:, None, :]
    return turned.reshape(row_count, heads_here * HEAD_DIM)


def norm_tangent(primal, tangent, gains):
    primal_f = primal.astype(jnp.float32)
    tangent_f = tangent.astype(jnp.float32)
    inverse = lax.rsqrt(jnp.mean(primal_f * primal_f, axis=1, keepdims=True) + EPSILON)
    cross = jnp.mean(primal_f * tangent_f, axis=1, keepdims=True)
    normed = primal_f * inverse * gains
    normed_tan = gains * (tangent_f * inverse - primal_f * inverse * inverse * inverse * cross)
    return (normed, normed_tan)


def prepare(proj_rows, tangent_rows, position_ids, norm_gain):
    cosine, sine_part = rope_angles(position_ids)
    query_n, query_dn = norm_tangent(proj_rows[0], tangent_rows[0], norm_gain[0])
    key_n, key_dn = norm_tangent(proj_rows[1], tangent_rows[1], norm_gain[1])
    queries = rotate(query_n, cosine, sine_part).astype(jnp.bfloat16)
    key_rows = rotate(key_n, cosine, sine_part).astype(jnp.bfloat16)
    query_tan = rotate(query_dn, cosine, sine_part).astype(jnp.bfloat16)
    key_tan = rotate(key_dn, cosine, sine_part).astype(jnp.bfloat16)
    return (queries, key_rows, proj_rows[2], query_tan, key_tan, tangent_rows[2])


def transposed_dot(left_side, right_side):
    return lax.dot_general(
        left_side, right_side, (((1,), (1,)), ((), ())), preferred_element_type=jnp.float32
    )


def attend_head(queries, key_rows, val_rows, query_tan, key_tan, val_tan):
    length = queries.shape[0]
    block_rows = min(512, length)
    blocks = length // block_rows
    factor = HEAD_DIM ** (-0.5)

    def one_block(inputs):
        query_block, query_tan_block = inputs
        scores = transposed_dot(query_block, key_rows) * factor
        shifted = scores - jnp.max(scores, axis=1, keepdims=True)
        weights = jnp.exp(shifted)
        probability = weights / jnp.sum(weights, axis=1, keepdims=True)
        prob_low = probability.astype(jnp.bfloat16)
        output = jnp.dot(prob_low, val_rows, preferred_element_type=jnp.float32)
        score_tan = (
            transposed_dot(query_tan_block, key_rows) + transposed_dot(query_block, key_tan)
        ) * factor
        weighted = probability * score_tan
        prob_tan = (weighted - probability * jnp.sum(weighted, axis=1, keepdims=True)).astype(
            jnp.bfloat16
        )
        output_tan = jnp.dot(prob_tan, val_rows, preferred_element_type=jnp.float32) + jnp.dot(
            prob_low, val_tan, preferred_element_type=jnp.float32
        )
        return (output.astype(jnp.bfloat16), output_tan.astype(jnp.bfloat16))

    width = queries.shape[1]
    results = lax.map(
        one_block,
        (queries.reshape(blocks, block_rows, width), query_tan.reshape(blocks, block_rows, width)),
    )
    return (results[0].reshape(length, width), results[1].reshape(length, width))


def attend_heads(queries, key_rows, val_rows, query_tan, key_tan, val_tan):
    length = queries.shape[0]
    heads_here = queries.shape[1] // HEAD_DIM

    def split_heads(matrix):
        return matrix.reshape(matrix.shape[0], heads_here, HEAD_DIM).transpose(1, 0, 2)

    def one_head(inputs):
        return attend_head(*inputs)

    stacked = tuple(
        (
            split_heads(matrix)
            for matrix in (queries, key_rows, val_rows, query_tan, key_tan, val_tan)
        )
    )
    outputs, outputs_tan = lax.map(one_head, stacked)
    return (
        outputs.transpose(1, 0, 2).reshape(length, heads_here * HEAD_DIM),
        outputs_tan.transpose(1, 0, 2).reshape(length, heads_here * HEAD_DIM),
    )


def embed_time(timestep, time_tangent):
    half_freq = FREQ // 2
    frequency = jnp.power(10000.0, -jnp.arange(half_freq, dtype=jnp.float32) / half_freq)
    angles = timestep.astype(jnp.float32)[:, None] * frequency[None, :]
    embedding = jnp.concatenate([jnp.cos(angles), jnp.sin(angles)], axis=1)
    embed_tan = (
        jnp.concatenate([-frequency * jnp.sin(angles), frequency * jnp.cos(angles)], axis=1)
        * time_tangent[:, None]
    )
    return (embedding.astype(jnp.bfloat16), embed_tan.astype(jnp.bfloat16))


def per_device(
    projections,
    projection_tangent,
    position_ids,
    norm_gain,
    out_weight,
    timestep,
    time_tangent,
    gate_weight,
    residual,
    residual_tangent,
):
    prepared = prepare(projections, projection_tangent, position_ids, norm_gain)
    stacked = jnp.stack(prepared)
    by_heads = lax.all_to_all(stacked, "head", split_axis=2, concat_axis=1, tiled=True)
    outputs, outputs_tan = attend_heads(
        by_heads[0], by_heads[1], by_heads[2], by_heads[3], by_heads[4], by_heads[5]
    )
    clip_index = lax.axis_index("dp")
    embedding, embed_tan = embed_time(timestep, time_tangent)
    full_gate = lax.all_gather(gate_weight, "dp", axis=0, tiled=True)
    own_embed = lax.dynamic_slice_in_dim(embedding, clip_index, 1, 0)
    own_tan = lax.dynamic_slice_in_dim(embed_tan, clip_index, 1, 0)
    gate_vec = jnp.dot(own_embed, full_gate, preferred_element_type=jnp.float32)[0]
    gate_tan = jnp.dot(own_tan, full_gate, preferred_element_type=jnp.float32)[0]
    col_weight = lax.all_gather(out_weight, "dp", axis=0, tiled=True)
    col_width = col_weight.shape[1]
    col_start = lax.axis_index("head") * col_width
    gate_cols = lax.dynamic_slice_in_dim(gate_vec, col_start, col_width, 0)
    gate_tan_cols = lax.dynamic_slice_in_dim(gate_tan, col_start, col_width, 0)
    row_weight = lax.all_to_all(col_weight, "head", split_axis=0, concat_axis=1, tiled=True)
    partial_out = jnp.dot(outputs, row_weight, preferred_element_type=jnp.float32)
    partial_tan = jnp.dot(outputs_tan, row_weight, preferred_element_type=jnp.float32)
    attended, attended_tan = (
        lax.psum_scatter(
            partial_out.astype(jnp.bfloat16), "head", scatter_dimension=1, tiled=True
        ).astype(jnp.float32),
        lax.psum_scatter(
            partial_tan.astype(jnp.bfloat16), "head", scatter_dimension=1, tiled=True
        ).astype(jnp.float32),
    )
    mixed_out = (residual.astype(jnp.float32) + gate_cols[None, :] * attended).astype(jnp.bfloat16)
    mixed_tan = (
        residual_tangent.astype(jnp.float32)
        + gate_tan_cols[None, :] * attended
        + gate_cols[None, :] * attended_tan
    ).astype(jnp.bfloat16)
    return (mixed_out, mixed_tan)


def solution(mesh):
    placed = (
        P(None, ("dp", "head"), None),
        P(None, ("dp", "head"), None),
        P(("dp", "head"), None),
        P(),
        P("dp", "head"),
        P(),
        P(),
        P("dp", None),
        P("dp", "head"),
        P("dp", "head"),
    )
    return jax.shard_map(
        per_device,
        mesh=mesh,
        in_specs=placed,
        out_specs=(P("dp", "head"), P("dp", "head")),
        check_vma=False,
    )
```

profile of v0, /device:TPU:10, one launch (start us, length us, event | category | flops | bytes accessed | tf_op | source)
XLA Modules:
  0.0 525.0 jit_solution(1467451048767944445)
XLA Ops:
  7.9 2.6 fusion.56
  10.9 2.9 fusion.55
  15.9 3.1 subtract_multiply_fusion.1
  19.0 1.9 multiply_multiply_fusion.2
  20.9 2.9 slice_negate_fusion.3
  24.2 1.5 copy.83
  25.7 1.6 mul.448
  28.5 3.0 subtract_multiply_fusion
  31.5 2.1 multiply_multiply_fusion.1
  33.6 2.9 slice_negate_fusion.2
  36.5 2.3 copy.81
  38.8 2.3 copy.84
  41.1 4.1 pad_maximum_fusion
  45.2 2.7 pad_maximum_fusion.1
  48.6 3.6 slice_negate_fusion.1
  52.2 1.5 pad_maximum_fusion.2
  53.7 1.7 slice_negate_fusion
  55.4 1.5 pad_maximum_fusion.3
  57.3 2.2 fusion.34
  59.7 1.0 copy-done.6
  62.0 19.2 %copy.54 = bf16[6,128,3072]{1,0,2:T(8,128)(2,1)} copy(bf16[6,128,3072]{1,2,0:T(8,128)(2,1)S(1)} %constant_dynamic-update-slice_fusion.2) | data formatting | bytes 9437184 | tf_op jit(solution)/shard_map/stack | solution.py:155
  81.3 5.7 %all-to-all-start = ((bf16[6,128,3072]{1,0,2:T(8,128)(2,1)}), bf16[6,128,3072]{1,0,2:T(8,128)(2,1)}, u32[]{:S(2)}, u32[]{:S(2)}) async-start(bf16[6,128,3072]{1,0,2:T(8,128)(2,1)} %copy.54), calls=%async_computation | async-start | bytes 12582912 | tf_op jit(solution)/shard_map/all_to_all | solution.py:156
  87.7 89.9 %all-to-all-done = bf16[6,128,3072]{1,0,2:T(8,128)(2,1)} async-done(((bf16[6,128,3072]{1,0,2:T(8,128)(2,1)}), bf16[6,128,3072]{1,0,2:T(8,128)(2,1)}, u32[]{:S(2)}, u32[]{:S(2)}) %all-to-all-start) | async-done | bytes 4718624 | tf_op jit(solution)/shard_map/all_to_all | solution.py:156
  177.6 5.8 %copy.86 = bf16[6,128,8,384]{1,2,3,0:T(8,128)(2,1)S(1)} copy(bf16[6,128,8,384]{1,0,3,2:T(8,128)(2,1)} %bitcast.29) | data formatting | bytes 9437184 | tf_op jit(solution)/shard_map/all_to_all | solution.py:156
  183.4 1.7 fusion.54
  185.2 1.8 reshape_squeeze.18
  187.0 2.2 reshape_squeeze.19
  189.2 2.2 reshape_squeeze.20
  191.4 2.2 reshape_squeeze.21
  193.6 1.2 reshape_squeeze.22
  194.8 1.2 reshape_squeeze.23
  196.0 7.3 %all-to-all-start.1 = ((bf16[8,384,640]{2,1,0:T(8,128)(2,1)}), bf16[8,384,640]{2,1,0:T(8,128)(2,1)}, u32[]{:S(2)}, u32[]{:S(2)}) async-start(bf16[8,384,640]{2,1,0:T(8,128)(2,1)} %bitcast.208), calls=%async_computation.1 | async-start | bytes 7864320 | tf_op jit(solution)/shard_map/all_to_all | solution.py:172
  203.4 45.5 %while.25 = (s32[]{:T(128)}, bf16[3,1024,128]{1,2,0:T(8,128)(2,1)}, bf16[3,1024,128]{1,2,0:T(8,128)(2,1)}, bf16[3,1024,128]{1,2,0:T(8,128)(2,1)S(1)}, bf16[3,102...) while((s32[]{:T(128)}, bf16[3,1024,128]{1,2,0:T(8,128)(2,1)}, ...), condition=%wide.region_10.11_spmd, body=%wide.region_4.10_spmd.sunk | while | flops 814414336 | bytes 36322140 | solution.py:123
  203.6 1.0 constant_dynamic-slice_fusion.13
  204.7 1.0 constant_dynamic-slice_fusion.14
  205.9 1.0 constant_dynamic-slice_fusion.15
  207.0 1.0 constant_dynamic-slice_fusion.16
  208.2 1.0 constant_dynamic-slice_fusion.17
  209.3 8.0 %while.26 = (s32[]{:T(128)}, bf16[2,512,128]{2,1,0:T(8,128)(2,1)S(1)}, bf16[2,512,128]{2,1,0:T(8,128)(2,1)S(1)}, bf16[2,512,128]{2,1,0:T(8,128)(2,1)S(1)}, bf16[...) while((s32[]{:T(128)}, ...), condition=%wide.region_9.9_spmd, body=%wide.region_5.8_spmd.sunk | while | flops 814414336 | bytes 27932792 | solution.py:100
  218.7 1.0 constant_dynamic-slice_fusion.13
  219.9 1.0 constant_dynamic-slice_fusion.14
  221.0 1.0 constant_dynamic-slice_fusion.15
  222.2 1.0 constant_dynamic-slice_fusion.16
  223.3 1.0 constant_dynamic-slice_fusion.17
  224.5 8.0 %while.26 = (s32[]{:T(128)}, bf16[2,512,128]{2,1,0:T(8,128)(2,1)S(1)}, bf16[2,512,128]{2,1,0:T(8,128)(2,1)S(1)}, bf16[2,512,128]{2,1,0:T(8,128)(2,1)S(1)}, bf16[...) while((s32[]{:T(128)}, ...), condition=%wide.region_9.9_spmd, body=%wide.region_5.8_spmd.sunk | while | flops 814414336 | bytes 27932792 | solution.py:100
  233.9 1.0 constant_dynamic-slice_fusion.13
  235.0 1.0 constant_dynamic-slice_fusion.14
  236.2 1.0 constant_dynamic-slice_fusion.15
  237.3 1.0 constant_dynamic-slice_fusion.16
  238.5 1.0 constant_dynamic-slice_fusion.17
  239.6 8.0 %while.26 = (s32[]{:T(128)}, bf16[2,512,128]{2,1,0:T(8,128)(2,1)S(1)}, bf16[2,512,128]{2,1,0:T(8,128)(2,1)S(1)}, bf16[2,512,128]{2,1,0:T(8,128)(2,1)S(1)}, bf16[...) while((s32[]{:T(128)}, ...), condition=%wide.region_9.9_spmd, body=%wide.region_5.8_spmd.sunk | while | flops 814414336 | bytes 27932792 | solution.py:100
  248.8 4.4 all-to-all-done.1
  253.2 6.3 %copy.63 = bf16[384,8,640]{0,2,1:T(8,128)(2,1)} copy(bf16[384,8,640]{2,0,1:T(8,128)(2,1)} %bitcast.40) | data formatting | bytes 7864320 | tf_op jit(solution)/shard_map/all_to_all | solution.py:172
  259.6 10.4 %convolution_convert_fusion.2 = bf16[1024,5120]{1,0:T(8,128)(2,1)} fusion(bf16[1024,384]{0,1:T(8,128)(2,1)S(1)} %bitcast.219, bf16[384,5120]{0,1:T(8,128)(2,1)} %bitcast.209), kind=kOutput, calls=%fused_computation.38 | convolution fusion | flops 4031774720 | bytes 15204352 | tf_op jit(solution)/shard_map/dot_general | solution.py:173
  270.0 14.4 %copy.65 = bf16[1024,5120]{0,1:T(8,128)(2,1)} copy(bf16[1024,5120]{1,0:T(8,128)(2,1)} %convolution_convert_fusion.2) | data formatting | bytes 20971520
  284.5 1.1 copy-done.14
  285.6 10.6 %convolution_convert_fusion.1 = bf16[1024,5120]{1,0:T(8,128)(2,1)} fusion(bf16[1024,384]{0,1:T(8,128)(2,1)S(1)} %bitcast.220, bf16[384,5120]{0,1:T(8,128)(2,1)} %bitcast.210), kind=kOutput, calls=%fused_computation.37 | convolution fusion | flops 4031774720 | bytes 15204352 | tf_op jit(solution)/shard_map/dot_general | solution.py:174
  296.2 14.5 %copy.67 = bf16[1024,5120]{0,1:T(8,128)(2,1)} copy(bf16[1024,5120]{1,0:T(8,128)(2,1)} %convolution_convert_fusion.1) | data formatting | bytes 20971520
  312.1 3.0 fusion.41
  315.7 83.1 %reduce-scatter.7.cloned.1.call-done = bf16[640,1024]{1,0:T(8,128)(2,1)} async-done(((bf16[5120,1024]{1,0:T(8,128)(2,1)}), bf16[640,1024]{1,0:T(8,128)(2,1)}) %reduce-scatter.7.cloned.1.call-update) | async-done | bytes 1310736
  398.8 1.7 copy.66
  400.5 111.9 %reduce-scatter.9.cloned.1.call-done = bf16[640,1024]{1,0:T(8,128)(2,1)} async-done(((bf16[5120,1024]{1,0:T(8,128)(2,1)}), bf16[640,1024]{1,0:T(8,128)(2,1)}) %reduce-scatter.9.cloned.1.call-update) | async-done | bytes 1310736
  512.4 1.7 copy.68
  514.1 4.2 fusion.26
  (156 shorter events, 40.3 us)
Async XLA Ops:
  7.2 188.9 %all-gather.5.cloned.1.call-start = ((), (), s32[]{:S(2)}) async-start(), calls=%async_computation.5 | async-start | bytes 4177920 | tf_op jit(solution)/shard_map/all_gather | solution.py:167
  13.8 0.7 copy-start.9
  27.3 1.1 copy-start.1
  33.6 2.9 copy-start.12
  33.6 2.9 copy-start.10
  41.1 4.1 copy-start.7
  41.1 4.1 copy-start.8
  52.2 1.5 copy-start.4
  53.7 3.2 copy-start.11
  55.4 1.8 copy-start.2
  55.4 1.9 copy-start.3
  59.5 1.1 copy-start.6
  60.8 1.2 copy-start.5
  81.3 96.3 %all-to-all-start = ((bf16[6,128,3072]{1,0,2:T(8,128)(2,1)}), bf16[6,128,3072]{1,0,2:T(8,128)(2,1)}, u32[]{:S(2)}, u32[]{:S(2)}) async-start(bf16[6,128,3072]{1,0,2:T(8,128)(2,1)} %copy.54), calls=%async_computation | async-start | bytes 12582912 | tf_op jit(solution)/shard_map/all_to_all | solution.py:156
  87.0 225.1 %all-gather.3.cloned.1.call-start = ((), (), s32[]{:S(2)}) async-start(), calls=%async_computation.4 | async-start | bytes 2785280 | tf_op jit(solution)/shard_map/all_gather | solution.py:162
  196.0 57.2 %all-to-all-start.1 = ((bf16[8,384,640]{2,1,0:T(8,128)(2,1)}), bf16[8,384,640]{2,1,0:T(8,128)(2,1)}, u32[]{:S(2)}, u32[]{:S(2)}) async-start(bf16[8,384,640]{2,1,0:T(8,128)(2,1)} %bitcast.208), calls=%async_computation.1 | async-start | bytes 7864320 | tf_op jit(solution)/shard_map/all_to_all | solution.py:172
  203.4 195.4 %reduce-scatter.7.cloned.1.call-start = ((), (), s32[]{:S(2)}) async-start(), calls=%async_computation.6 | async-start | bytes 11796480
  253.2 6.4 %copy-start.13 = (bf16[3,1024,128]{1,2,0:T(8,128)(2,1)S(1)}, bf16[3,1024,128]{1,2,0:T(8,128)(2,1)}, u32[]{:S(2)}) copy-start(bf16[3,1024,128]{1,2,0:T(8,128)(2,1)} %get-tuple-element.98) | copy-start | bytes 2359300
  284.5 1.1 copy-start.14
  284.5 227.9 %reduce-scatter.9.cloned.1.call-start = ((), (), s32[]{:S(2)}) async-start(), calls=%async_computation.7 | async-start | bytes 11796480
  310.7 0.7 copy-start.15
  310.7 0.7 copy-start.16
  312.1 3.1 copy-start
Sparse Core Ops, SparseCore 0:
  10.5 55.5 all-gather.4
  90.3 98.9 all-gather.2
  284.6 114.1 reduce-scatter.6
  401.1 111.2 reduce-scatter.8
where the time goes:
time: 535 us; the launch traced here: 525 us
  waiting for transfers between devices  291 us (54%)
  local copies, waits for them, and re-layouts  119 us (22%)
  other arithmetic  44.6 us (8%)
  matrix products  42.3 us (8%)
  between operations  14.3 us (3%)
  starting transfers between devices  13.2 us (2%)
    unnamed x6, waiting for transfers between devices  196 us
    all_to_all x1, waiting for transfers between devices, per_device(): lax.all_to_all(stacked, 'head', split_axis=2, concat_axis=1, tiled=True)  89.9 us
    unnamed x49, local copies, waits for them, and re-layouts  44.8 us
    another operation x2, local copies, waits for them, and re-layouts, per_device(): stacked = jnp.stack(prepared)  19.3 us
    dynamic_slice x36, local copies, waits for them, and re-layouts, attend_heads(): outputs, outputs_tan = lax.map(one_head, stacked)  17.7 us
    neg x4, other arithmetic, rotate(): -pairs_view[..., 1]  11.1 us
    another operation x6, local copies, waits for them, and re-layouts, split_heads(): matrix.reshape(matrix.shape[0], heads_here, HEAD_DIM).transpose(1, 0, 2)  10.8 us
  transfers between devices with their start and end apart: 6, of which 4 were waited for; matrix products, arithmetic and copies ran while one was open for 37% of the time, Pallas kernels for 0%

commit v1 on v0

v1 whole, which is shorter than its diff:
```python
import math

import jax
import jax.numpy as jnp
import numpy as np
from jax import lax
from jax.experimental import pallas as pl
from jax.experimental.pallas import tpu as pltpu
from jax.sharding import PartitionSpec as P

HEAD_DIM = 128
ATT_W = 3072
EPSILON = 1e-06
MESH = pl.DeviceIdType.MESH
BF = jnp.bfloat16
F32 = jnp.float32

X = 4
ROWS = 128
SEQ = 1024
HALF = 512
GW = 384
COLS = 640
FACTOR = HEAD_DIM ** (-0.5)

ORDER = ((1, 0), (0, 1), (0, 3), (1, 2), (0, 2), (1, 1), (1, 3))


def constants():
    pair_count = HEAD_DIM // 2
    height_pairs = HEAD_DIM // 6
    time_pairs = pair_count - 2 * height_pairs
    j = np.arange(pair_count)
    local = np.where(
        j < time_pairs,
        j,
        np.where(j < time_pairs + height_pairs, j - time_pairs, j - time_pairs - height_pairs),
    )
    span = np.where(j < time_pairs, time_pairs, height_pairs)
    rope = np.repeat(np.power(10000.0, -local / span), 2)
    clock = np.power(10000.0, -np.arange(128) / 128)
    rows = np.zeros((8, 128), np.float32)
    rows[0] = rope
    rows[1] = clock
    return rows, 2 * time_pairs, 2 * (time_pairs + height_pairs)


CONST, LANE_ROW, LANE_COL = constants()


def nt_dot(a, b):
    return lax.dot_general(a, b, (((1,), (1,)), ((), ())), preferred_element_type=F32)


def kernel(
    proj,
    tan,
    pos,
    gain,
    wout,
    time,
    ttan,
    wgate,
    res,
    rtan,
    const,
    out,
    otan,
    raw,
    sv,
    sq,
    recv,
    ob,
    pb,
    wall,
    gall,
    resv,
    po,
    pr,
    load_sem,
    res_sem,
    v_send,
    v_recv,
    q_send,
    q_recv,
    pre_send,
    pre_recv,
    w_send,
    w_recv,
    g_send,
    g_recv,
    x_send,
    x_recv,
    y_send,
    y_recv,
):
    dp = lax.axis_index("dp")
    head = lax.axis_index("head")
    y, x = head // X, lax.rem(head, X)
    yh, z, c = dp // 8, lax.rem(dp // 2, 4), lax.rem(dp, 2)
    partner = {"dp": dp, "head": (1 - y) * X + x}
    right = {"dp": dp, "head": y * X + lax.rem(x + 1, X)}
    left = {"dp": dp, "head": y * X + lax.rem(x + 3, X)}
    xl, xr = lax.rem(x + 3, X), lax.rem(x + 1, X)
    other_core = {"dp": dp + 1 - 2 * c, "head": head}

    def z_peer(d):
        return {"dp": yh * 8 + lax.rem(z + d, 4) * 2 + c, "head": head}

    def y_peer(yl):
        return {"dp": (1 - yh) * 8 + z * 2 + c, "head": yl * X + x}

    def send(src, dst, ssem, rsem, to):
        pltpu.make_async_remote_copy(
            src_ref=src,
            dst_ref=dst,
            send_sem=ssem,
            recv_sem=rsem,
            device_id=to,
            device_id_type=MESH,
        ).start()

    def local(src, dst, sem):
        pltpu.make_async_copy(src, dst, sem).start()

    def wait(ref, sem):
        pltpu.make_async_copy(ref, ref, sem).wait()

    for h in range(3):

        def load_v(g, _, h=h):
            col = pl.ds(pl.multiple_of(g * GW + h * 128, 128), 128)
            local(proj.at[2, :, col], sv.at[h, g, :, pl.ds(0, 128)], load_sem.at[h])
            local(tan.at[2, :, col], sv.at[h, g, :, pl.ds(128, 128)], load_sem.at[h])
            return 0

        lax.fori_loop(0, 8, load_v, 0)
    local(proj.at[pl.ds(0, 2)], raw.at[0], load_sem.at[3])
    local(tan.at[pl.ds(0, 2)], raw.at[1], load_sem.at[3])
    local(wout, wall.at[y, yh, z, c], w_recv.at[0])
    local(
        wgate.at[:, pl.ds(pl.multiple_of(head * COLS, 128), COLS)],
        gall.at[yh, z, c],
        g_recv.at[0],
    )
    local(res, resv.at[0], res_sem)
    local(rtan, resv.at[1], res_sem)

    barrier = pltpu.get_barrier_semaphore()
    for dy, dx in ORDER:
        to = {"dp": dp, "head": lax.rem(y + dy, 2) * X + lax.rem(x + dx, X)}
        pl.semaphore_signal(barrier, inc=1, device_id=to, device_id_type=MESH)
    for d in (1, 2, 3):
        pl.semaphore_signal(barrier, inc=1, device_id=z_peer(d), device_id_type=MESH)
    pl.semaphore_signal(barrier, inc=1, device_id=other_core, device_id_type=MESH)
    for yl in (0, 1):
        pl.semaphore_signal(barrier, inc=1, device_id=y_peer(yl), device_id_type=MESH)
    pl.semaphore_wait(barrier, 13)

    for to in (partner, y_peer(0), y_peer(1)):
        send(wout, wall.at[y, yh, z, c], w_send.at[0], w_recv.at[0], to)
    mine = pl.ds(pl.multiple_of(head * ROWS, ROWS), ROWS)
    for h in range(3):
        wait(sv.at[h], load_sem.at[h])
        for dy, dx in ORDER:
            ty, tx = lax.rem(y + dy, 2), lax.rem(x + dx, X)
            g = ty * X + tx
            send(
                sv.at[h, g],
                recv.at[h, 2, mine],
                v_send.at[h],
                v_recv.at[h],
                {"dp": dp, "head": g},
            )
        local(sv.at[h, head], recv.at[h, 2, mine], v_recv.at[h])
    send(
        wgate.at[:, pl.ds(pl.multiple_of(head * COLS, 128), COLS)],
        gall.at[yh, z, c],
        g_send.at[0],
        g_recv.at[0],
        {"dp": (1 - yh) * 8 + z * 2 + c, "head": head},
    )

    lane = lax.broadcasted_iota(jnp.int32, (ROWS, 128), 1)
    ids = pos[...].astype(F32)
    chosen = jnp.where(
        lane < LANE_ROW, ids[:, 0:1], jnp.where(lane < LANE_COL, ids[:, 1:2], ids[:, 2:3])
    )
    angle = chosen * const[0:1, :]
    cosine = jnp.cos(angle)
    even = lax.rem(lane, 2) == 0
    sine = jnp.where(even, -jnp.sin(angle), jnp.sin(angle))

    def rotate(m):
        swapped = jnp.where(even, pltpu.roll(m, 127, 1), pltpu.roll(m, 1, 1))
        return (m * cosine + swapped * sine).astype(BF)

    wait(raw, load_sem.at[3])
    stats = []
    for a in (0, 1):

        def add(i, carry, a=a):
            square, cross = carry
            col = pl.ds(pl.multiple_of(i * 128, 128), 128)
            q = raw[0, a, :, col].astype(F32)
            dq = raw[1, a, :, col].astype(F32)
            return square + q * q, cross + q * dq

        zero = jnp.zeros((ROWS, 128), F32)
        square, cross = lax.fori_loop(0, ATT_W // 128, add, (zero, zero))
        r = lax.rsqrt(jnp.sum(square, axis=1, keepdims=True) / ATT_W + EPSILON)
        cr = jnp.sum(cross, axis=1, keepdims=True) / ATT_W
        stats.append((r, r * r * r * cr))

    for h in range(3):

        def prepare(i, _, h=h):
            ty, tx = lax.rem(y + i // X, 2), lax.rem(x + i, X)
            g = ty * X + tx
            col = pl.ds(pl.multiple_of(g * GW + h * 128, 128), 128)
            for a in (0, 1):
                r, rc = stats[a]
                q = raw[0, a, :, col].astype(F32)
                dq = raw[1, a, :, col].astype(F32)
                gn = gain[a : a + 1, col]
                n = rotate(q * r * gn)
                dn = rotate(gn * (dq * r - q * rc))
                if a == 0:
                    sq[h, g, 0, :, 0:128] = dn
                    sq[h, g, 0, :, 128:256] = n
                else:
                    sq[h, g, 1, :, 0:128] = n
                    sq[h, g, 1, :, 128:256] = dn

            @pl.when(i > 0)
            def _():
                send(
                    sq.at[h, g],
                    recv.at[h, pl.ds(0, 2), mine],
                    q_send.at[h],
                    q_recv.at[h],
                    {"dp": dp, "head": g},
                )

            return 0

        lax.fori_loop(0, 8, prepare, 0)
        local(sq.at[h, head], recv.at[h, pl.ds(0, 2), mine], q_recv.at[h])

    wait(wall.at[:, :, z, c], w_recv.at[0])
    wait(gall.at[:, z, c], g_recv.at[0])
    for d in (1, 3, 2):
        send(wall.at[:, :, z, c], wall.at[:, :, z, c], w_send.at[1], w_recv.at[1], z_peer(d))
        send(gall.at[:, z, c], gall.at[:, z, c], g_send.at[1], g_recv.at[1], z_peer(d))

    def attend(h, block):
        rows = pl.ds(pl.multiple_of(block * 256, 256), 256)
        qd = recv[h, 0, rows, :]
        kd = recv[h, 1]
        s = nt_dot(qd[:, 128:], kd[:, :128])
        ds = nt_dot(qd, kd)
        top = jnp.max(s, axis=1, keepdims=True)
        e = jnp.exp2((s - top) * (FACTOR * math.log2(math.e)))
        inv = 1.0 / jnp.sum(e, axis=1, keepdims=True)
        mu = jnp.sum(e * ds, axis=1, keepdims=True) * inv
        t = (e * (ds - mu)).astype(BF)
        vd = recv[h, 2]
        both = jnp.dot(e.astype(BF), vd, preferred_element_type=F32)
        turn = jnp.dot(t, vd[:, :128], preferred_element_type=F32)
        o = both[:, :128] * inv
        do = (both[:, 128:] + turn * FACTOR) * inv
        return o.astype(BF), do.astype(BF)

    def x_unit(rb, part):
        width = 256 if part == 0 else 128
        col = pl.ds(pl.multiple_of(x * GW + part * 256, 128), width)
        k = rb * 2 + part
        src = ob.at[rb, :, :, :, col]
        send(src, src, x_send.at[0], x_recv.at[0, k], right)
        send(src, src, x_send.at[1], x_recv.at[1, k], left)

    def forward(rb, part):
        width = 256 if part == 0 else 128
        k = rb * 2 + part
        col = pl.ds(pl.multiple_of(xl * GW + part * 256, 128), width)
        wait(ob.at[rb, :, :, :, col], x_recv.at[0, k])
        src = ob.at[rb, :, 0, :, col]
        send(src, src, x_send.at[2], x_recv.at[2, k], right)
        col = pl.ds(pl.multiple_of(xr * GW + part * 256, 128), width)
        wait(ob.at[rb, :, :, :, col], x_recv.at[1, k])
        src = ob.at[rb, :, 1, :, col]
        send(src, src, x_send.at[3], x_recv.at[3, k], left)

    for h in range(3):
        wait(recv.at[h, 2], v_recv.at[h])
        wait(recv.at[h, pl.ds(0, 2)], q_recv.at[h])
        own_col = pl.ds(pl.multiple_of(x * GW + h * 128, 128), 128)

        def for_partner(j, _, h=h):
            o, do = attend(h, (1 - y) * 2 + j)
            for i in (0, 1):
                pb[h, j * 2 + i, 0] = o[i * 128 : (i + 1) * 128]
                pb[h, j * 2 + i, 1] = do[i * 128 : (i + 1) * 128]
            return 0

        def for_self(j, _, h=h):
            o, do = attend(h, y * 2 + j)
            for i in (0, 1):
                ob[j * 2 + i, y, 0, :, own_col] = o[i * 128 : (i + 1) * 128]
                ob[j * 2 + i, y, 1, :, own_col] = do[i * 128 : (i + 1) * 128]
            return 0

        if h == 2:
            wait(ob.at[:, 0, :, :, pl.ds(0, 128)], pre_recv.at[0])
            wait(ob.at[:, 0, :, :, pl.ds(0, 128)], pre_recv.at[1])
            for rb in (0, 1):
                x_unit(rb, 0)
        lax.fori_loop(0, 2, for_partner, 0)
        send(pb.at[h], ob.at[:, y, :, :, own_col], pre_send.at[h], pre_recv.at[h], partner)
        lax.fori_loop(0, 2, for_self, 0)

    wait(wall.at[:, :, pl.ds(0, 3), c], w_recv.at[1])
    wait(gall.at[:, pl.ds(0, 3), c], g_recv.at[1])
    send(wall.at[:, :, :, c], wall.at[:, :, :, c], w_send.at[2], w_recv.at[2], other_core)
    send(gall.at[:, :, c], gall.at[:, :, c], g_send.at[2], g_recv.at[2], other_core)

    wait(ob.at[:, 0, :, :, pl.ds(0, 128)], pre_recv.at[2])
    x_unit(0, 1)
    x_unit(1, 1)
    for rb in (2, 3):
        x_unit(rb, 0)
        x_unit(rb, 1)

    wait(wall.at[:, :, :, 1 - c], w_recv.at[2])
    wait(gall.at[:, :, 1 - c], g_recv.at[2])
    moment = time[dp].astype(F32)
    speed = ttan[dp]
    freq = const[1:2, :]
    cos_t, sin_t = jnp.cos(moment * freq), jnp.sin(moment * freq)
    row = lax.broadcasted_iota(jnp.int32, (16, 256), 0)
    emb = jnp.concatenate([cos_t, sin_t], axis=1)
    demb = jnp.concatenate([-freq * sin_t, freq * cos_t], axis=1) * speed
    embs = jnp.where(row == 0, emb, jnp.where(row == 1, demb, 0.0)).astype(BF)
    gates = jnp.dot(embs, gall[...].reshape(256, COLS), preferred_element_type=F32)
    gate, dgate = gates[0:1], gates[1:2]

    wait(resv, res_sem)

    def finish(rows, attn, dattn):
        out[rows, :] = (resv[0, rows, :].astype(F32) + gate * attn).astype(BF)
        otan[rows, :] = (resv[1, rows, :].astype(F32) + dgate * attn + gate * dattn).astype(BF)

    def project(rb, yl):
        total = None
        for gy in (0, 1):
            term = jnp.dot(
                ob[rb, gy].reshape(256, 1536),
                wall[yl, gy].reshape(1536, COLS),
                preferred_element_type=F32,
            )
            total = term if total is None else total + term
        return total

    def forwards(rb, _):
        for part, width in ((0, 256), (1, 128)):
            k = rb * 2 + part
            col = pl.ds(pl.multiple_of(xl * GW + part * 256, 128), width)
            wait(ob.at[rb, :, :, :, col], x_recv.at[0, k])
            src = ob.at[rb, :, 0, :, col]
            send(src, src, x_send.at[2], x_recv.at[2, k], right)
            col = pl.ds(pl.multiple_of(xr * GW + part * 256, 128), width)
            wait(ob.at[rb, :, :, :, col], x_recv.at[1, k])
            src = ob.at[rb, :, 1, :, col]
            send(src, src, x_send.at[3], x_recv.at[3, k], left)
        return 0

    forwards(0, 0)

    def row_block(rb, _):
        @pl.when(rb < 3)
        def _():
            forwards(rb + 1, 0)

        for part, width in ((0, 256), (1, 128)):
            k = rb * 2 + part
            wait(ob.at[rb, :, 0, :, pl.ds(0, width)], x_recv.at[2, k])
            wait(ob.at[rb, :, 1, :, pl.ds(0, width)], x_recv.at[3, k])
        total = project(rb, 1 - y)
        po[rb] = total.astype(BF)
        send(po.at[rb], pr.at[rb], y_send.at[rb], y_recv.at[rb], partner)
        total = project(rb, y)
        rows = pl.ds(pl.multiple_of(y * HALF + rb * 128, 128), 128)
        finish(rows, total[:128], total[128:])
        return 0

    lax.fori_loop(0, 4, row_block, 0)

    def partner_block(rb, _):
        wait(pr.at[rb], y_recv.at[rb])
        rows = pl.ds(pl.multiple_of((1 - y) * HALF + rb * 128, 128), 128)
        finish(rows, pr[rb, 0:128].astype(F32), pr[rb, 128:256].astype(F32))
        return 0

    lax.fori_loop(0, 4, partner_block, 0)

    for h in range(3):
        wait(sv.at[h, pl.ds(0, 7)], v_send.at[h])
        wait(sq.at[h, pl.ds(0, 7)], q_send.at[h])
        wait(pb.at[h], pre_send.at[h])
    wait(wall.at[0, 0, pl.ds(0, 3), 0], w_send.at[0])
    wait(wall.at[:, :, pl.ds(0, 3), 0], w_send.at[1])
    wait(wall.at[:, :, :, 0], w_send.at[2])
    wait(gall.at[0, 0, 0], g_send.at[0])
    wait(gall.at[:, pl.ds(0, 3), 0], g_send.at[1])
    wait(gall.at[:, :, 0], g_send.at[2])
    wait(ob.at[:, :, :, :, pl.ds(0, GW)], x_send.at[0])
    wait(ob.at[:, :, :, :, pl.ds(0, GW)], x_send.at[1])
    wait(ob.at[:, :, 0, :, pl.ds(0, GW)], x_send.at[2])
    wait(ob.at[:, :, 1, :, pl.ds(0, GW)], x_send.at[3])
    for rb in range(4):
        wait(po.at[rb], y_send.at[rb])


def per_device(
    projections,
    projection_tangent,
    position_ids,
    norm_gain,
    out_weight,
    timestep,
    time_tangent,
    gate_weight,
    residual,
    residual_tangent,
):
    anywhere = pl.BlockSpec(memory_space=pl.ANY)
    vmem = pl.BlockSpec(memory_space=pltpu.VMEM)
    smem = pl.BlockSpec(memory_space=pltpu.SMEM)
    dma = pltpu.SemaphoreType.DMA
    shape = jax.ShapeDtypeStruct((SEQ, COLS), BF)
    return pl.pallas_call(
        kernel,
        out_shape=(shape, shape),
        in_specs=[
            anywhere,
            anywhere,
            vmem,
            vmem,
            anywhere,
            smem,
            smem,
            anywhere,
            anywhere,
            anywhere,
            vmem,
        ],
        out_specs=(vmem, vmem),
        scratch_shapes=[
            pltpu.VMEM((2, 2, ROWS, ATT_W), BF),
            pltpu.VMEM((3, 8, ROWS, 256), BF),
            pltpu.VMEM((3, 8, 2, ROWS, 256), BF),
            pltpu.VMEM((3, 3, SEQ, 256), BF),
            pltpu.VMEM((4, 2, 2, ROWS, 1536), BF),
            pltpu.VMEM((3, 4, 2, ROWS, 128), BF),
            pltpu.VMEM((2, 2, 4, 2, 192, COLS), BF),
            pltpu.VMEM((2, 4, 2, 16, COLS), BF),
            pltpu.VMEM((2, SEQ, COLS), BF),
            pltpu.VMEM((4, 256, COLS), BF),
            pltpu.VMEM((4, 256, COLS), BF),
            dma((4,)),
            dma,
            dma((3,)),
            dma((3,)),
            dma((3,)),
            dma((3,)),
            dma((3,)),
            dma((3,)),
            dma((3,)),
            dma((3,)),
            dma((3,)),
            dma((3,)),
            dma((4,)),
            dma((4, 8)),
            dma((4,)),
            dma((4,)),
        ],
        compiler_params=pltpu.CompilerParams(
            collective_id=0, has_side_effects=True, vmem_limit_bytes=60 * 2**20
        ),
    )(
        projections,
        projection_tangent,
        position_ids,
        norm_gain,
        out_weight,
        timestep,
        time_tangent,
        gate_weight,
        residual,
        residual_tangent,
        jnp.asarray(CONST),
    )


def solution(mesh):
    placed = (
        P(None, ("dp", "head"), None),
        P(None, ("dp", "head"), None),
        P(("dp", "head"), None),
        P(),
        P("dp", "head"),
        P(),
        P(),
        P("dp", None),
        P("dp", "head"),
        P("dp", "head"),
    )
    return jax.shard_map(
        per_device,
        mesh=mesh,
        in_specs=placed,
        out_specs=(P("dp", "head"), P("dp", "head")),
        check_vma=False,
    )
```

time: 535 us -> 163 us (0.30); the launches traced: 525 us -> 162 us
  waiting for transfers between devices: 291 us -> 0 us
  Pallas kernels: 0 us -> 157 us
  local copies, waits for them, and re-layouts: 119 us -> 5.06 us
  other arithmetic: 44.6 us -> 0 us
  matrix products: 42.3 us -> 0 us
  between operations: 14.3 us -> 0.65 us
  starting transfers between devices: 13.2 us -> 0 us
    unnamed x6 -> x0, waiting for transfers between devices: 196 us -> none
    pallas_call x0 -> x1, Pallas kernels: none -> 157 us  [per_device(): pl.pallas_call(kernel, out_shape=(shape, shape), in_specs=[anywhere, anyw...]
    all_to_all x2 -> x0, waiting for transfers between devices: 94.3 us -> none  [the longest x1 89.9 us: per_device(): lax.all_to_all(stacked, 'head', split_axis=2, concat_axis=1, tiled=True)]
    dot_general x40 -> x0, matrix products: 42.3 us -> none  [the longest x1 10.6 us: per_device(): jnp.dot(outputs_tan, row_weight, preferred_element_type=jnp.float32)]
    unnamed x49 -> x5, local copies, waits for them, and re-layouts: 44.8 us -> 5.06 us
    another operation x8 -> x0, local copies, waits for them, and re-layouts: 30.1 us -> none  [the longest x2 19.3 us: per_device(): stacked = jnp.stack(prepared)]
    dynamic_slice x39 -> x0, local copies, waits for them, and re-layouts: 18.4 us -> none  [the longest x36 17.7 us: attend_heads(): outputs, outputs_tan = lax.map(one_head, stacked)]
    all_to_all x2 -> x0, starting transfers between devices: 13.1 us -> none  [the longest x1 7.34 us: per_device(): lax.all_to_all(col_weight, 'head', split_axis=0, concat_axis=1, tiled=True)]
  transfers between devices with their start and end apart: 6 -> 0, of which waited for: 4 -> 0; matrix products, arithmetic and copies ran while one was open for 37% -> 0% of each run, Pallas kernels for 0% -> 0%
where the time goes in v1:
time: 163 us; the launch traced here: 162 us
  Pallas kernels  157 us (96%)
  local copies, waits for them, and re-layouts  5.06 us (3%)
    pallas_call x1, Pallas kernels, per_device(): pl.pallas_call(kernel, out_shape=(shape, shape), in_specs=[anywhere, anyw...  157 us
    unnamed x5, local copies, waits for them, and re-layouts  5.06 us

profile of v1, /device:TPU:10, one launch (start us, length us, event | category | flops | bytes accessed | tf_op | source)
XLA Modules:
  0.0 162.5 jit_solution(11929229835316520950)
XLA Ops:
  0.6 1.4 copy.13.pos
  2.0 156.8 %shard_map.122 = (bf16[1024,640]{1,0:T(8,128)(2,1)}, bf16[1024,640]{1,0:T(8,128)(2,1)}) custom-call(bf16[3,128,3072]{2,1,0:T(8,128)(2,1)} %proj.1, bf16[3,128,3072]{2,1,0:T(8,128)(2,1)} %tan.1, s32[128,3]{1,0:T(8,128)} %copy.13.pos, f32[2,3072]{1,0:T(2,128)} %gain.1, bf16[192,640]{1,0:T(8,128)(2,1)} %wout.1, s32[16]{0:T(128)} %time.1, f32[16]{0:T(128)} %ttan.1, ...), custom_call_target="tpu_custom_call" | custom-call | tf_op jit(solution)/shard_map/pallas_call | solution.py:441
  158.8 0.0 copy-start
  158.8 2.6 %copy.16 = bf16[1024,640]{1,0:T(8,128)(2,1)} copy(bf16[1024,640]{1,0:T(8,128)(2,1)} %get-tuple-element.4) | data formatting | bytes 2621440
  161.4 0.0 copy-done
  161.4 1.1 copy.17
Async XLA Ops:
  158.8 2.6 %copy-start = (bf16[1024,640]{1,0:T(8,128)(2,1)S(1)}, bf16[1024,640]{1,0:T(8,128)(2,1)}, u32[]{:S(2)}) copy-start(bf16[1024,640]{1,0:T(8,128)(2,1)} %get-tuple-element.5) | copy-start | bytes 3932164

commit v2 on v1

v2 whole, which is shorter than its diff:
```python
import math

import jax
import jax.numpy as jnp
import numpy as np
from jax import lax
from jax.experimental import pallas as pl
from jax.experimental.pallas import tpu as pltpu
from jax.sharding import PartitionSpec as P

HEAD_DIM = 128
ATT_W = 3072
EPSILON = 1e-06
MESH = pl.DeviceIdType.MESH
BF = jnp.bfloat16
F32 = jnp.float32

X = 4
ROWS = 128
SEQ = 1024
HALF = 512
GW = 384
COLS = 640
FACTOR = HEAD_DIM ** (-0.5)

PIECES = ((0, 0, 128), (1, 0, 128), (2, 0, 128), (3, 0, 64), (3, 64, 64))
PARTS = ((0, 256), (256, 128), (0, 384))

ORDER = ((1, 0), (0, 1), (0, 3), (1, 2), (0, 2), (1, 1), (1, 3))


def constants():
    pair_count = HEAD_DIM // 2
    height_pairs = HEAD_DIM // 6
    time_pairs = pair_count - 2 * height_pairs
    j = np.arange(pair_count)
    local = np.where(
        j < time_pairs,
        j,
        np.where(j < time_pairs + height_pairs, j - time_pairs, j - time_pairs - height_pairs),
    )
    span = np.where(j < time_pairs, time_pairs, height_pairs)
    rope = np.repeat(np.power(10000.0, -local / span), 2)
    clock = np.power(10000.0, -np.arange(128) / 128)
    rows = np.zeros((8, 128), np.float32)
    rows[0] = rope
    rows[1] = clock
    return rows, 2 * time_pairs, 2 * (time_pairs + height_pairs)


CONST, LANE_ROW, LANE_COL = constants()


def nt_dot(a, b):
    return lax.dot_general(a, b, (((1,), (1,)), ((), ())), preferred_element_type=F32)


def kernel(
    proj,
    tan,
    pos_hbm,
    gain_hbm,
    wout,
    time_hbm,
    ttan_hbm,
    wgate,
    res,
    rtan,
    const_hbm,
    out,
    otan,
    pos,
    gain,
    time,
    ttan,
    const,
    raw,
    sv,
    sq,
    recv,
    ob,
    pb,
    wall,
    gall,
    resv,
    outv,
    po,
    pr,
    small_sem,
    load_sem,
    res_sem,
    out_sem,
    v_send,
    v_recv,
    q_send,
    q_recv,
    pre_send,
    pre_recv,
    wy_send,
    wy_recv,
    wz_send,
    wz_recv,
    wc_send,
    wc_recv,
    g_send,
    g_recv,
    x_send,
    x_recv,
    y_send,
    y_recv,
):
    dp = lax.axis_index("dp")
    head = lax.axis_index("head")
    y, x = head // X, lax.rem(head, X)
    yh, z, c = dp // 8, lax.rem(dp // 2, 4), lax.rem(dp, 2)
    partner = {"dp": dp, "head": (1 - y) * X + x}
    right = {"dp": dp, "head": y * X + lax.rem(x + 1, X)}
    left = {"dp": dp, "head": y * X + lax.rem(x + 3, X)}
    xl, xr = lax.rem(x + 3, X), lax.rem(x + 1, X)
    other_core = {"dp": dp + 1 - 2 * c, "head": head}

    def z_peer(d):
        return {"dp": yh * 8 + lax.rem(z + d, 4) * 2 + c, "head": head}

    def send(src, dst, ssem, rsem, to):
        pltpu.make_async_remote_copy(
            src_ref=src,
            dst_ref=dst,
            send_sem=ssem,
            recv_sem=rsem,
            device_id=to,
            device_id_type=MESH,
        ).start()

    def local(src, dst, sem):
        pltpu.make_async_copy(src, dst, sem).start()

    def wait(ref, sem):
        pltpu.make_async_copy(ref, ref, sem).wait()

    def sends_v(h):
        for dy, dx in ORDER:
            g = lax.rem(y + dy, 2) * X + lax.rem(x + dx, X)
            to = {"dp": dp, "head": g}
            send(sv.at[h, g], recv.at[h, 2, mine], v_send.at[h], v_recv.at[h], to)
        local(sv.at[h, head], recv.at[h, 2, mine], v_recv.at[h])

    def send_q(h, g):
        to = {"dp": dp, "head": g}
        send(sq.at[h, g], recv.at[h, pl.ds(0, 2), mine], q_send.at[h], q_recv.at[h], to)

    def sends_q(h):
        for dy, dx in ORDER:
            send_q(h, lax.rem(y + dy, 2) * X + lax.rem(x + dx, X))
        local(sq.at[h, head], recv.at[h, pl.ds(0, 2), mine], q_recv.at[h])

    def shard(s):
        return wall.at[y if s in (0, 2) else 1 - y, yh if s in (0, 1) else 1 - yh]

    def y_chip(s):
        row = yh if s in (0, 1) else 1 - yh
        return {
            "dp": row * 8 + z * 2 + c,
            "head": (y if s in (0, 2) else 1 - y) * X + x,
        }

    def shard_along_z(s):
        for d in (1, 3, 2):
            src = shard(s).at[z, c]
            send(src, src, wz_send.at[s], wz_recv.at[s], z_peer(d))

    def shard_to_core(s):
        wait(shard(s).at[pl.ds(0, 3), c], wz_recv.at[s])
        src = shard(s).at[:, c]
        send(src, src, wc_send.at[s], wc_recv.at[s], other_core)

    mine = pl.ds(pl.multiple_of(head * ROWS, ROWS), ROWS)
    gate_cols = wgate.at[:, pl.ds(pl.multiple_of(head * COLS, 128), COLS)]

    for h in range(3):

        def load_v(g, _, h=h):
            col = pl.ds(pl.multiple_of(g * GW + h * 128, 128), 128)
            local(proj.at[2, :, col], sv.at[h, g, :, pl.ds(0, 128)], load_sem.at[h])
            local(tan.at[2, :, col], sv.at[h, g, :, pl.ds(128, 128)], load_sem.at[h])
            return 0

        lax.fori_loop(0, 8, load_v, 0)
    local(wout, shard(0).at[z, c], wy_recv.at[0])
    small = ((pos_hbm, pos), (gain_hbm, gain), (time_hbm, time), (ttan_hbm, ttan), (const_hbm, const))
    for i, (src, dst) in enumerate(small):
        local(src, dst, small_sem.at[i])
    local(proj.at[pl.ds(0, 2)], raw.at[0], load_sem.at[3])
    local(tan.at[pl.ds(0, 2)], raw.at[1], load_sem.at[3])
    local(gate_cols, gall.at[yh, z, c], g_recv.at[0])
    local(res, resv.at[0], res_sem)
    local(rtan, resv.at[1], res_sem)

    barrier = pltpu.get_barrier_semaphore()
    for dy, dx in ORDER:
        to = {"dp": dp, "head": lax.rem(y + dy, 2) * X + lax.rem(x + dx, X)}
        pl.semaphore_signal(barrier, inc=1, device_id=to, device_id_type=MESH)
    for to in (z_peer(1), z_peer(2), z_peer(3), other_core, y_chip(2), y_chip(3)):
        pl.semaphore_signal(barrier, inc=1, device_id=to, device_id_type=MESH)
    pl.semaphore_wait(barrier, 13)

    wait(shard(0).at[z, c], wy_recv.at[0])
    src = shard(0).at[z, c]
    send(src, src, wy_send.at[3], wy_recv.at[3], y_chip(3))
    shard_along_z(0)
    for h in (0, 1):
        wait(sv.at[h], load_sem.at[h])
        sends_v(h)
    send(gate_cols, gall.at[yh, z, c], g_send.at[0], g_recv.at[0], y_chip(2))

    for i, (_, dst) in enumerate(small):
        wait(dst, small_sem.at[i])

    line = lax.broadcasted_iota(jnp.int32, (128, ROWS), 0)
    ids = pos[...].astype(F32)
    chosen = jnp.where(
        line < LANE_ROW, ids[0:1, :], jnp.where(line < LANE_COL, ids[1:2, :], ids[2:3, :])
    )
    angle = jnp.transpose(chosen) * const[0:1, :]
    lane = lax.broadcasted_iota(jnp.int32, (ROWS, 128), 1)
    even = lax.rem(lane, 2) == 0
    cosine, sine = jnp.cos(angle), jnp.sin(angle)
    sine = jnp.where(even, -sine, sine)

    def rotate(m):
        swapped = jnp.where(even, pltpu.roll(m, 127, 1), pltpu.roll(m, 1, 1))
        return (m * cosine + swapped * sine).astype(BF)

    wait(raw, load_sem.at[3])
    stats = []
    for a in (0, 1):

        def add(i, carry, a=a):
            square, cross = carry
            col = pl.ds(pl.multiple_of(i * 128, 128), 128)
            q = raw[0, a, :, col].astype(F32)
            dq = raw[1, a, :, col].astype(F32)
            return square + q * q, cross + q * dq

        zero = jnp.zeros((ROWS, 128), F32)
        square, cross = lax.fori_loop(0, ATT_W // 128, add, (zero, zero))
        r = lax.rsqrt(jnp.sum(square, axis=1, keepdims=True) / ATT_W + EPSILON)
        cr = jnp.sum(cross, axis=1, keepdims=True) / ATT_W
        stats.append((r, r * r * r * cr))

    for h in range(3):

        def prepare(i, _, h=h):
            g = lax.rem(y + i // X, 2) * X + lax.rem(x + i, X)
            col = pl.ds(pl.multiple_of(g * GW + h * 128, 128), 128)
            for a in (0, 1):
                r, rc = stats[a]
                q = raw[0, a, :, col].astype(F32)
                dq = raw[1, a, :, col].astype(F32)
                gn = gain[a : a + 1, col]
                n = rotate(q * r * gn)
                dn = rotate(gn * (dq * r - q * rc))
                sq[h, g, a, :, 0:128] = dn if a == 0 else n
                sq[h, g, a, :, 128:256] = n if a == 0 else dn

            if h == 0:

                @pl.when(i > 0)
                def _():
                    send_q(h, g)

            return 0

        lax.fori_loop(0, 8, prepare, 0)
        if h == 0:
            local(sq.at[h, head], recv.at[h, pl.ds(0, 2), mine], q_recv.at[h])

    def attend(h, block):
        rows = pl.ds(pl.multiple_of(block * 256, 256), 256)
        qd = recv[h, 0, rows, :]
        kd = recv[h, 1]
        s = nt_dot(qd[:, 128:], kd[:, :128])
        ds = nt_dot(qd, kd)
        top = jnp.max(s, axis=1, keepdims=True)
        e = jnp.exp2((s - top) * (FACTOR * math.log2(math.e)))
        inv = 1.0 / jnp.sum(e, axis=1, keepdims=True)
        mu = jnp.sum(e * ds, axis=1, keepdims=True) * inv
        t = (e * (ds - mu)).astype(BF)
        vd = recv[h, 2]
        both = jnp.dot(e.astype(BF), vd, preferred_element_type=F32)
        turn = jnp.dot(t, vd[:, :128], preferred_element_type=F32)
        o = both[:, :128] * inv
        do = (both[:, 128:] + turn * FACTOR) * inv
        return o.astype(BF), do.astype(BF)

    def swap(h, pair):
        two = pl.ds(pair * 2, 2)
        col = pl.ds(pl.multiple_of(x * GW + h * 128, 128), 128)
        k = h * 2 + pair
        send(pb.at[h, two], ob.at[two, y, :, :, col], pre_send.at[k], pre_recv.at[k], partner)

    def swapped(h, pair):
        wait(ob.at[pl.ds(pair * 2, 2), 0, :, :, pl.ds(0, 128)], pre_recv.at[h * 2 + pair])

    def attention(h):
        own_col = pl.ds(pl.multiple_of(x * GW + h * 128, 128), 128)

        def for_partner(j, _):
            o, do = attend(h, (1 - y) * 2 + j)
            for i in (0, 1):
                pb[h, j * 2 + i, 0] = o[i * 128 : (i + 1) * 128]
                pb[h, j * 2 + i, 1] = do[i * 128 : (i + 1) * 128]
            return 0

        def for_self(j, _):
            o, do = attend(h, y * 2 + j)
            for i in (0, 1):
                ob[j * 2 + i, y, 0, :, own_col] = o[i * 128 : (i + 1) * 128]
                ob[j * 2 + i, y, 1, :, own_col] = do[i * 128 : (i + 1) * 128]
            return 0

        if h < 2:
            lax.fori_loop(0, 2, for_partner, 0)
            swap(h, 0)
        else:
            for_partner(0, 0)
            for earlier, pair in ((2, 0), (0, 1), (1, 1)):
                swap(earlier, pair)
            for_partner(1, 0)
            swap(2, 1)
        lax.fori_loop(0, 2, for_self, 0)

    def unit(p, part, which, from_x):
        rb, first, rows = PIECES[p]
        skip, width = PARTS[part]
        col = pl.ds(pl.multiple_of(from_x * GW + skip, 128), width)
        group = y if which == 0 else 1 - y
        k = p * 4 + part % 2 * 2 + which
        return ob.at[rb, group, :, pl.ds(first, rows), col], k

    def x_unit(p, part, which):
        src, k = unit(p, part, which, x)
        send(src, src, x_send.at[0], x_recv.at[0, k], right)
        send(src, src, x_send.at[1], x_recv.at[1, k], left)

    def forward(p, part, which):
        src, k = unit(p, part, which, xl)
        wait(src, x_recv.at[0, k])
        send(src.at[0], src.at[0], x_send.at[2], x_recv.at[2, k], right)
        src, k = unit(p, part, which, xr)
        wait(src, x_recv.at[1, k])
        send(src.at[1], src.at[1], x_send.at[3], x_recv.at[3, k], left)

    def arrived(p):
        for which, parts in ((0, (0, 1) if p < 3 else (2,)), (1, (0, 1) if p < 2 else (2,))):
            for part in parts:
                src, k = unit(p, part, which, x)
                wait(src.at[0], x_recv.at[2, k])
                wait(src.at[1], x_recv.at[3, k])

    wait(shard(3).at[z, c], wy_recv.at[3])
    shard_along_z(3)

    wait(recv.at[0, 2], v_recv.at[0])
    wait(recv.at[1, 2], v_recv.at[1])
    sends_q(1)
    wait(sv.at[2], load_sem.at[2])
    sends_v(2)

    shard_to_core(0)
    wait(gall.at[:, z, c], g_recv.at[0])
    for d in (1, 3, 2):
        send(gall.at[:, z, c], gall.at[:, z, c], g_send.at[1], g_recv.at[1], z_peer(d))

    wait(recv.at[0, pl.ds(0, 2)], q_recv.at[0])
    sends_q(2)
    src = shard(0).at[z, c]
    send(src, src, wy_send.at[1], wy_recv.at[1], y_chip(1))
    attention(0)

    shard_to_core(3)
    wait(recv.at[1, pl.ds(0, 2)], q_recv.at[1])
    attention(1)
    x_unit(0, 0, 0)
    x_unit(1, 0, 0)

    wait(gall.at[:, pl.ds(0, 3), c], g_recv.at[1])
    send(gall.at[:, :, c], gall.at[:, :, c], g_send.at[2], g_recv.at[2], other_core)

    wait(recv.at[2, 2], v_recv.at[2])
    wait(recv.at[2, pl.ds(0, 2)], q_recv.at[2])
    attention(2)
    x_unit(0, 1, 0)
    x_unit(1, 1, 0)
    wait(shard(1).at[z, c], wy_recv.at[1])
    shard_along_z(1)
    src = shard(1).at[z, c]
    send(src, src, wy_send.at[2], wy_recv.at[2], y_chip(3))
    forward(0, 0, 0)
    swapped(0, 0)
    swapped(1, 0)
    x_unit(0, 0, 1)
    forward(1, 0, 0)
    wait(shard(2).at[z, c], wy_recv.at[2])
    shard_along_z(2)
    forward(0, 1, 0)
    swapped(2, 0)
    x_unit(0, 1, 1)
    x_unit(1, 0, 1)
    forward(0, 0, 1)
    shard_to_core(1)
    forward(1, 1, 0)
    x_unit(1, 1, 1)
    forward(0, 1, 1)
    x_unit(2, 0, 0)
    x_unit(2, 1, 0)
    forward(1, 0, 1)
    forward(1, 1, 1)
    for h in range(3):
        swapped(h, 1)
    x_unit(2, 2, 1)

    wait(gall.at[:, :, 1 - c], g_recv.at[2])
    moment = time[dp].astype(F32)
    speed = ttan[dp]
    freq = const[1:2, :]
    cos_t, sin_t = jnp.cos(moment * freq), jnp.sin(moment * freq)
    row = lax.broadcasted_iota(jnp.int32, (16, 256), 0)
    emb = jnp.concatenate([cos_t, sin_t], axis=1)
    demb = jnp.concatenate([-freq * sin_t, freq * cos_t], axis=1) * speed
    embs = jnp.where(row == 0, emb, jnp.where(row == 1, demb, 0.0)).astype(BF)
    gates = jnp.dot(embs, gall[...].reshape(256, COLS), preferred_element_type=F32)
    gate, dgate = gates[0:1], gates[1:2]

    for s in (1, 3):
        wait(shard(s).at[:, 1 - c], wc_recv.at[s])
    wait(resv, res_sem)

    def finish(rows, attn, dattn):
        outv[0, rows, :] = (resv[0, rows, :].astype(F32) + gate * attn).astype(BF)
        outv[1, rows, :] = (resv[1, rows, :].astype(F32) + dgate * attn + gate * dattn).astype(BF)
        local(outv.at[0, rows], out.at[rows], out_sem)
        local(outv.at[1, rows], otan.at[rows], out_sem)

    def project(p, yl):
        rb, first, rows = PIECES[p]
        total = None
        for gy in (0, 1):
            term = jnp.dot(
                ob[rb, gy, :, first : first + rows, :].reshape(2 * rows, 1536),
                wall[yl, gy].reshape(1536, COLS),
                preferred_element_type=F32,
            )
            total = term if total is None else total + term
        return total

    def own_piece(p):
        rb, first, rows = PIECES[p]
        total = project(p, y)
        start = pl.multiple_of(y * HALF + rb * 128 + first, 64)
        finish(pl.ds(start, rows), total[:rows], total[rows:])

    for p, (rb, first, rows) in enumerate(PIECES):
        arrived(p)
        total = project(p, 1 - y)
        both = pl.ds(0, 2 * rows)
        po[p, both] = total.astype(BF)
        send(po.at[p, both], pr.at[p, both], y_send.at[p], y_recv.at[p], partner)
        if p == 0:
            forward(2, 0, 0)
            x_unit(3, 2, 0)
            forward(2, 1, 0)
            x_unit(3, 2, 1)
            forward(2, 2, 1)
            shard_to_core(2)
        elif p == 1:
            x_unit(4, 2, 0)
            forward(3, 2, 0)
            x_unit(4, 2, 1)
            forward(3, 2, 1)
            for s in (0, 2):
                wait(shard(s).at[:, 1 - c], wc_recv.at[s])
            own_piece(0)
        elif p == 2:
            forward(4, 2, 0)
            forward(4, 2, 1)
            own_piece(1)
        elif p == 3:
            own_piece(2)
        else:
            own_piece(3)
            own_piece(4)

    for p, (rb, first, rows) in enumerate(PIECES):
        wait(pr.at[p, pl.ds(0, 2 * rows)], y_recv.at[p])
        start = pl.multiple_of((1 - y) * HALF + rb * 128 + first, 64)
        finish(
            pl.ds(start, rows),
            pr[p, 0:rows].astype(F32),
            pr[p, rows : 2 * rows].astype(F32),
        )

    for h in range(3):
        wait(sv.at[h, pl.ds(0, 7)], v_send.at[h])
        wait(sq.at[h, pl.ds(0, 7)], q_send.at[h])
        for pair in (0, 1):
            wait(pb.at[h, pl.ds(pair * 2, 2)], pre_send.at[h * 2 + pair])
    for s in range(4):
        if s > 0:
            wait(shard(0).at[0, 0], wy_send.at[s])
        wait(shard(0).at[pl.ds(0, 3), 0], wz_send.at[s])
        wait(shard(0).at[:, 0], wc_send.at[s])
    wait(gall.at[0, 0, 0], g_send.at[0])
    wait(gall.at[:, pl.ds(0, 3), 0], g_send.at[1])
    wait(gall.at[:, :, 0], g_send.at[2])
    wait(ob.at[:, :, :, :, pl.ds(0, GW)], x_send.at[0])
    wait(ob.at[:, :, :, :, pl.ds(0, GW)], x_send.at[1])
    wait(ob.at[:, :, 0, :, pl.ds(0, GW)], x_send.at[2])
    wait(ob.at[:, :, 1, :, pl.ds(0, GW)], x_send.at[3])
    for p, (_, _, rows) in enumerate(PIECES):
        wait(po.at[p, pl.ds(0, 2 * rows)], y_send.at[p])
    wait(outv, out_sem)


def per_device(
    projections,
    projection_tangent,
    position_ids,
    norm_gain,
    out_weight,
    timestep,
    time_tangent,
    gate_weight,
    residual,
    residual_tangent,
):
    anywhere = pl.BlockSpec(memory_space=pl.ANY)
    dma = pltpu.SemaphoreType.DMA
    shape = jax.ShapeDtypeStruct((SEQ, COLS), BF)
    return pl.pallas_call(
        kernel,
        out_shape=(shape, shape),
        in_specs=[pl.BlockSpec(memory_space=pltpu.HBM)] * 11,
        out_specs=(anywhere, anywhere),
        scratch_shapes=[
            pltpu.VMEM((3, ROWS), jnp.int32),
            pltpu.VMEM((2, ATT_W), F32),
            pltpu.SMEM((16,), jnp.int32),
            pltpu.SMEM((16,), F32),
            pltpu.VMEM((8, 128), F32),
            pltpu.VMEM((2, 2, ROWS, ATT_W), BF),
            pltpu.VMEM((3, 8, ROWS, 256), BF),
            pltpu.VMEM((3, 8, 2, ROWS, 256), BF),
            pltpu.VMEM((3, 3, SEQ, 256), BF),
            pltpu.VMEM((4, 2, 2, ROWS, 1536), BF),
            pltpu.VMEM((3, 4, 2, ROWS, 128), BF),
            pltpu.VMEM((2, 2, 4, 2, 192, COLS), BF),
            pltpu.VMEM((2, 4, 2, 16, COLS), BF),
            pltpu.VMEM((2, SEQ, COLS), BF),
            pltpu.VMEM((2, SEQ, COLS), BF),
            pltpu.VMEM((5, 256, COLS), BF),
            pltpu.VMEM((5, 256, COLS), BF),
            dma((5,)),
            dma((4,)),
            dma,
            dma,
            dma((3,)),
            dma((3,)),
            dma((3,)),
            dma((3,)),
            dma((6,)),
            dma((6,)),
            dma((4,)),
            dma((4,)),
            dma((4,)),
            dma((4,)),
            dma((4,)),
            dma((4,)),
            dma((3,)),
            dma((3,)),
            dma((4,)),
            dma((4, 20)),
            dma((5,)),
            dma((5,)),
        ],
        compiler_params=pltpu.CompilerParams(
            collective_id=0, has_side_effects=True, vmem_limit_bytes=56 * 2**20
        ),
    )(
        projections,
        projection_tangent,
        position_ids.T,
        norm_gain,
        out_weight,
        timestep,
        time_tangent,
        gate_weight,
        residual,
        residual_tangent,
        jnp.asarray(CONST),
    )


def solution(mesh):
    placed = (
        P(None, ("dp", "head"), None),
        P(None, ("dp", "head"), None),
        P(("dp", "head"), None),
        P(),
        P("dp", "head"),
        P(),
        P(),
        P("dp", None),
        P("dp", "head"),
        P("dp", "head"),
    )
    return jax.shard_map(
        per_device,
        mesh=mesh,
        in_specs=placed,
        out_specs=(P("dp", "head"), P("dp", "head")),
        check_vma=False,
    )
```

time: 163 us -> 126 us (0.77)
  Pallas kernels: 157 us -> 121 us
    pallas_call x1, Pallas kernels: 157 us -> 121 us  [per_device(): pl.pallas_call(kernel, out_shape=(shape, shape), in_specs=[pl.BlockSpec(m...]
    unnamed x5 -> x4, local copies, waits for them, and re-layouts: 5.06 us -> 3.65 us
where the time goes in v2:
time: 126 us; the launch traced here: 125 us
  Pallas kernels  121 us (96%)
  local copies, waits for them, and re-layouts  3.65 us (3%)
    pallas_call x1, Pallas kernels, per_device(): pl.pallas_call(kernel, out_shape=(shape, shape), in_specs=[pl.BlockSpec(m...  121 us
    unnamed x4, local copies, waits for them, and re-layouts  3.65 us

profile of v2, /device:TPU:10, one launch (start us, length us, event | category | flops | bytes accessed | tf_op | source)
XLA Modules:
  0.0 124.9 jit_solution(8191127661244575016)
XLA Ops:
  0.6 120.6 %shard_map.122 = (bf16[1024,640]{1,0:T(8,128)(2,1)}, bf16[1024,640]{1,0:T(8,128)(2,1)}) custom-call(bf16[3,128,3072]{2,1,0:T(8,128)(2,1)} %proj.1, bf16[3,128,3072]{2,1,0:T(8,128)(2,1)} %tan.1, s32[3,128]{1,0:T(4,128)} %bitcast.1, f32[2,3072]{1,0:T(2,128)} %gain_hbm.1, bf16[192,640]{1,0:T(8,128)(2,1)} %wout.1, s32[16]{0:T(128)} %time_hbm.1, f32[16]{0:T(128)} %ttan_hbm.1, ...), custom_call_target="tpu_custom_call" | custom-call | tf_op jit(solution)/shard_map/pallas_call | solution.py:540
  121.2 0.0 copy-start
  121.2 2.6 %copy.15 = bf16[1024,640]{1,0:T(8,128)(2,1)} copy(bf16[1024,640]{1,0:T(8,128)(2,1)} %get-tuple-element.4) | data formatting | bytes 2621440
  123.8 0.0 copy-done
  123.8 1.1 copy.16
Async XLA Ops:
  121.2 2.6 %copy-start = (bf16[1024,640]{1,0:T(8,128)(2,1)S(1)}, bf16[1024,640]{1,0:T(8,128)(2,1)}, u32[]{:S(2)}) copy-start(bf16[1024,640]{1,0:T(8,128)(2,1)} %get-tuple-element.5) | copy-start | bytes 3932164

commit v3 on v2

--- a/solution.py
+++ b/solution.py
@@ -23,7 +23,15 @@
 COLS = 640
 FACTOR = HEAD_DIM ** (-0.5)
 
-PIECES = ((0, 0, 128), (1, 0, 128), (2, 0, 128), (3, 0, 64), (3, 64, 64))
+PIECES = (
+    (0, 0, 128),
+    (1, 0, 128),
+    (2, 0, 64),
+    (2, 64, 64),
+    (3, 0, 64),
+    (3, 64, 32),
+    (3, 96, 32),
+)
 PARTS = ((0, 256), (256, 128), (0, 384))
 
 ORDER = ((1, 0), (0, 1), (0, 3), (1, 2), (0, 2), (1, 1), (1, 3))
@@ -106,6 +114,7 @@
     g_recv,
     x_send,
     x_recv,
+    f_recv,
     y_send,
     y_recv,
 ):
@@ -142,12 +151,12 @@
         for dy, dx in ORDER:
             g = lax.rem(y + dy, 2) * X + lax.rem(x + dx, X)
             to = {"dp": dp, "head": g}
-            send(sv.at[h, g], recv.at[h, 2, mine], v_send.at[h], v_recv.at[h], to)
-        local(sv.at[h, head], recv.at[h, 2, mine], v_recv.at[h])
+            send(sv.at[h, g], recv.at[h, 2, mine], v_send, (v_recv if h < 2 else q_recv).at[h], to)
+        local(sv.at[h, head], recv.at[h, 2, mine], (v_recv if h < 2 else q_recv).at[h])
 
     def send_q(h, g):
         to = {"dp": dp, "head": g}
-        send(sq.at[h, g], recv.at[h, pl.ds(0, 2), mine], q_send.at[h], q_recv.at[h], to)
+        send(sq.at[h, g], recv.at[h, pl.ds(0, 2), mine], q_send, q_recv.at[h], to)
 
     def sends_q(h):
         for dy, dx in ORDER:
@@ -167,12 +176,12 @@
     def shard_along_z(s):
         for d in (1, 3, 2):
             src = shard(s).at[z, c]
-            send(src, src, wz_send.at[s], wz_recv.at[s], z_peer(d))
+            send(src, src, wz_send, wz_recv.at[s], z_peer(d))
 
     def shard_to_core(s):
         wait(shard(s).at[pl.ds(0, 3), c], wz_recv.at[s])
         src = shard(s).at[:, c]
-        send(src, src, wc_send.at[s], wc_recv.at[s], other_core)
+        send(src, src, wc_send, wc_recv.at[s % 2], other_core)
 
     mine = pl.ds(pl.multiple_of(head * ROWS, ROWS), ROWS)
     gate_cols = wgate.at[:, pl.ds(pl.multiple_of(head * COLS, 128), COLS)]
@@ -181,8 +190,8 @@
 
         def load_v(g, _, h=h):
             col = pl.ds(pl.multiple_of(g * GW + h * 128, 128), 128)
-            local(proj.at[2, :, col], sv.at[h, g, :, pl.ds(0, 128)], load_sem.at[h])
-            local(tan.at[2, :, col], sv.at[h, g, :, pl.ds(128, 128)], load_sem.at[h])
+            local(proj.at[2, :, col], sv.at[h, g, :, pl.ds(0, 128)], load_sem.at[0])
+            local(tan.at[2, :, col], sv.at[h, g, :, pl.ds(128, 128)], load_sem.at[0])
             return 0
 
         lax.fori_loop(0, 8, load_v, 0)
@@ -190,8 +199,8 @@
     small = ((pos_hbm, pos), (gain_hbm, gain), (time_hbm, time), (ttan_hbm, ttan), (const_hbm, const))
     for i, (src, dst) in enumerate(small):
         local(src, dst, small_sem.at[i])
-    local(proj.at[pl.ds(0, 2)], raw.at[0], load_sem.at[3])
-    local(tan.at[pl.ds(0, 2)], raw.at[1], load_sem.at[3])
+    local(proj.at[pl.ds(0, 2)], raw.at[0], load_sem.at[1])
+    local(tan.at[pl.ds(0, 2)], raw.at[1], load_sem.at[1])
     local(gate_cols, gall.at[yh, z, c], g_recv.at[0])
     local(res, resv.at[0], res_sem)
     local(rtan, resv.at[1], res_sem)
@@ -206,11 +215,11 @@
 
     wait(shard(0).at[z, c], wy_recv.at[0])
     src = shard(0).at[z, c]
-    send(src, src, wy_send.at[3], wy_recv.at[3], y_chip(3))
+    send(src, src, wy_send, wy_recv.at[3], y_chip(3))
     shard_along_z(0)
-    for h in (0, 1):
-        wait(sv.at[h], load_sem.at[h])
-        sends_v(h)
+    wait(sv, load_sem.at[0])
+    sends_v(0)
+    sends_v(1)
     send(gate_cols, gall.at[yh, z, c], g_send.at[0], g_recv.at[0], y_chip(2))
 
     for i, (_, dst) in enumerate(small):
@@ -231,7 +240,7 @@
         swapped = jnp.where(even, pltpu.roll(m, 127, 1), pltpu.roll(m, 1, 1))
         return (m * cosine + swapped * sine).astype(BF)
 
-    wait(raw, load_sem.at[3])
+    wait(raw, load_sem.at[1])
     stats = []
     for a in (0, 1):
 
@@ -296,11 +305,12 @@
     def swap(h, pair):
         two = pl.ds(pair * 2, 2)
         col = pl.ds(pl.multiple_of(x * GW + h * 128, 128), 128)
-        k = h * 2 + pair
-        send(pb.at[h, two], ob.at[two, y, :, :, col], pre_send.at[k], pre_recv.at[k], partner)
-
-    def swapped(h, pair):
-        wait(ob.at[pl.ds(pair * 2, 2), 0, :, :, pl.ds(0, 128)], pre_recv.at[h * 2 + pair])
+        k = 2 if pair == 1 else h // 2
+        send(pb.at[h, two], ob.at[two, y, :, :, col], pre_send, pre_recv.at[k], partner)
+
+    def swapped(k):
+        width = (256, 128, 384)[k]
+        wait(ob.at[pl.ds(0, 2), 0, :, :, pl.ds(0, width)], pre_recv.at[k])
 
     def attention(h):
         own_col = pl.ds(pl.multiple_of(x * GW + h * 128, 128), 128)
@@ -335,28 +345,26 @@
         skip, width = PARTS[part]
         col = pl.ds(pl.multiple_of(from_x * GW + skip, 128), width)
         group = y if which == 0 else 1 - y
-        k = p * 4 + part % 2 * 2 + which
+        k = p * 4 + part * 2 + which if p < 2 else 4 + p * 2 + which
         return ob.at[rb, group, :, pl.ds(first, rows), col], k
 
     def x_unit(p, part, which):
         src, k = unit(p, part, which, x)
-        send(src, src, x_send.at[0], x_recv.at[0, k], right)
-        send(src, src, x_send.at[1], x_recv.at[1, k], left)
+        send(src, src, x_send, x_recv.at[k], right)
+        send(src, src, x_send, x_recv.at[k], left)
 
     def forward(p, part, which):
+        rb, first, rows = PIECES[p]
         src, k = unit(p, part, which, xl)
-        wait(src, x_recv.at[0, k])
-        send(src.at[0], src.at[0], x_send.at[2], x_recv.at[2, k], right)
+        two = ob.at[rb, :, :, pl.ds(first, rows), pl.ds(0, PARTS[part][1])]
+        wait(two, x_recv.at[k])
+        send(src.at[0], src.at[0], x_send, f_recv.at[p], right)
         src, k = unit(p, part, which, xr)
-        wait(src, x_recv.at[1, k])
-        send(src.at[1], src.at[1], x_send.at[3], x_recv.at[3, k], left)
+        send(src.at[1], src.at[1], x_send, f_recv.at[p], left)
 
     def arrived(p):
-        for which, parts in ((0, (0, 1) if p < 3 else (2,)), (1, (0, 1) if p < 2 else (2,))):
-            for part in parts:
-                src, k = unit(p, part, which, x)
-                wait(src.at[0], x_recv.at[2, k])
-                wait(src.at[1], x_recv.at[3, k])
+        rb, first, rows = PIECES[p]
+        wait(ob.at[rb, :, :, pl.ds(first, rows), pl.ds(0, GW)], f_recv.at[p])
 
     wait(shard(3).at[z, c], wy_recv.at[3])
     shard_along_z(3)
@@ -364,7 +372,6 @@
     wait(recv.at[0, 2], v_recv.at[0])
     wait(recv.at[1, 2], v_recv.at[1])
     sends_q(1)
-    wait(sv.at[2], load_sem.at[2])
     sends_v(2)
 
     shard_to_core(0)
@@ -375,7 +382,7 @@
     wait(recv.at[0, pl.ds(0, 2)], q_recv.at[0])
     sends_q(2)
     src = shard(0).at[z, c]
-    send(src, src, wy_send.at[1], wy_recv.at[1], y_chip(1))
+    send(src, src, wy_send, wy_recv.at[1], y_chip(1))
     attention(0)
 
     shard_to_core(3)
@@ -387,24 +394,22 @@
     wait(gall.at[:, pl.ds(0, 3), c], g_recv.at[1])
     send(gall.at[:, :, c], gall.at[:, :, c], g_send.at[2], g_recv.at[2], other_core)
 
-    wait(recv.at[2, 2], v_recv.at[2])
-    wait(recv.at[2, pl.ds(0, 2)], q_recv.at[2])
+    wait(recv.at[2], q_recv.at[2])
     attention(2)
     x_unit(0, 1, 0)
     x_unit(1, 1, 0)
     wait(shard(1).at[z, c], wy_recv.at[1])
     shard_along_z(1)
     src = shard(1).at[z, c]
-    send(src, src, wy_send.at[2], wy_recv.at[2], y_chip(3))
+    send(src, src, wy_send, wy_recv.at[2], y_chip(3))
     forward(0, 0, 0)
-    swapped(0, 0)
-    swapped(1, 0)
+    swapped(0)
     x_unit(0, 0, 1)
     forward(1, 0, 0)
     wait(shard(2).at[z, c], wy_recv.at[2])
     shard_along_z(2)
     forward(0, 1, 0)
-    swapped(2, 0)
+    swapped(1)
     x_unit(0, 1, 1)
     x_unit(1, 0, 1)
     forward(0, 0, 1)
@@ -412,13 +417,12 @@
     forward(1, 1, 0)
     x_unit(1, 1, 1)
     forward(0, 1, 1)
-    x_unit(2, 0, 0)
-    x_unit(2, 1, 0)
+    x_unit(2, 2, 0)
     forward(1, 0, 1)
     forward(1, 1, 1)
-    for h in range(3):
-        swapped(h, 1)
+    swapped(2)
     x_unit(2, 2, 1)
+    x_unit(3, 2, 0)
 
     wait(gall.at[:, :, 1 - c], g_recv.at[2])
     moment = time[dp].astype(F32)
@@ -432,8 +436,7 @@
     gates = jnp.dot(embs, gall[...].reshape(256, COLS), preferred_element_type=F32)
     gate, dgate = gates[0:1], gates[1:2]
 
-    for s in (1, 3):
-        wait(shard(s).at[:, 1 - c], wc_recv.at[s])
+    wait(wall.at[1 - y, :, :, 1 - c], wc_recv.at[1])
     wait(resv, res_sem)
 
     def finish(rows, attn, dattn):
@@ -442,8 +445,7 @@
         local(outv.at[0, rows], out.at[rows], out_sem)
         local(outv.at[1, rows], otan.at[rows], out_sem)
 
-    def project(p, yl):
-        rb, first, rows = PIECES[p]
+    def project(rb, first, rows, yl):
         total = None
         for gy in (0, 1):
             term = jnp.dot(
@@ -454,72 +456,83 @@
             total = term if total is None else total + term
         return total
 
-    def own_piece(p):
-        rb, first, rows = PIECES[p]
-        total = project(p, y)
-        start = pl.multiple_of(y * HALF + rb * 128 + first, 64)
-        finish(pl.ds(start, rows), total[:rows], total[rows:])
+    def own_block(rb):
+        total = project(rb, 0, ROWS, y)
+        start = pl.multiple_of(y * HALF + rb * ROWS, ROWS)
+        finish(pl.ds(start, ROWS), total[:ROWS], total[ROWS:])
 
     for p, (rb, first, rows) in enumerate(PIECES):
         arrived(p)
-        total = project(p, 1 - y)
+        total = project(rb, first, rows, 1 - y)
         both = pl.ds(0, 2 * rows)
         po[p, both] = total.astype(BF)
-        send(po.at[p, both], pr.at[p, both], y_send.at[p], y_recv.at[p], partner)
+        send(po.at[p, both], pr.at[p, both], y_send, y_recv.at[p], partner)
         if p == 0:
-            forward(2, 0, 0)
-            x_unit(3, 2, 0)
-            forward(2, 1, 0)
+            forward(2, 2, 0)
             x_unit(3, 2, 1)
-            forward(2, 2, 1)
             shard_to_core(2)
         elif p == 1:
+            forward(2, 2, 1)
             x_unit(4, 2, 0)
             forward(3, 2, 0)
             x_unit(4, 2, 1)
+            wait(wall.at[y, :, :, 1 - c], wc_recv.at[0])
+            own_block(0)
+        elif p == 2:
             forward(3, 2, 1)
-            for s in (0, 2):
-                wait(shard(s).at[:, 1 - c], wc_recv.at[s])
-            own_piece(0)
-        elif p == 2:
+            x_unit(5, 2, 0)
             forward(4, 2, 0)
+            x_unit(5, 2, 1)
+            own_block(1)
+        elif p == 3:
             forward(4, 2, 1)
-            own_piece(1)
-        elif p == 3:
-            own_piece(2)
-        else:
-            own_piece(3)
-            own_piece(4)
+            x_unit(6, 2, 0)
+            forward(5, 2, 0)
+            x_unit(6, 2, 1)
+        elif p == 4:
+            forward(5, 2, 1)
+            forward(6, 2, 0)
+            forward(6, 2, 1)
+            own_block(2)
+        elif p == 6:
+            own_block(3)
+
+    wait(sv.at[:, pl.ds(0, 7)], v_send)
+    wait(sq.at[:, pl.ds(0, 7)], q_send)
+    wait(pb, pre_send)
+    wait(wall.at[0, 0, pl.ds(0, 3), 0], wy_send)
+    wait(wall.at[:, :, pl.ds(0, 3), 0], wz_send)
+    wait(wall.at[:, :, :, 0], wc_send)
+    wait(gall.at[0, 0, 0], g_send.at[0])
+    wait(gall.at[:, pl.ds(0, 3), 0], g_send.at[1])
+    wait(gall.at[:, :, 0], g_send.at[2])
+    wait(ob.at[:, :, :, :, pl.ds(0, 3 * GW)], x_send)
 
     for p, (rb, first, rows) in enumerate(PIECES):
         wait(pr.at[p, pl.ds(0, 2 * rows)], y_recv.at[p])
-        start = pl.multiple_of((1 - y) * HALF + rb * 128 + first, 64)
+        start = pl.multiple_of((1 - y) * HALF + rb * 128 + first, 32)
         finish(
             pl.ds(start, rows),
             pr[p, 0:rows].astype(F32),
             pr[p, rows : 2 * rows].astype(F32),
         )
-
-    for h in range(3):
-        wait(sv.at[h, pl.ds(0, 7)], v_send.at[h])
-        wait(sq.at[h, pl.ds(0, 7)], q_send.at[h])
-        for pair in (0, 1):
-            wait(pb.at[h, pl.ds(pair * 2, 2)], pre_send.at[h * 2 + pair])
-    for s in range(4):
-        if s > 0:
-            wait(shard(0).at[0, 0], wy_send.at[s])
-        wait(shard(0).at[pl.ds(0, 3), 0], wz_send.at[s])
-        wait(shard(0).at[:, 0], wc_send.at[s])
-    wait(gall.at[0, 0, 0], g_send.at[0])
-    wait(gall.at[:, pl.ds(0, 3), 0], g_send.at[1])
-    wait(gall.at[:, :, 0], g_send.at[2])
-    wait(ob.at[:, :, :, :, pl.ds(0, GW)], x_send.at[0])
-    wait(ob.at[:, :, :, :, pl.ds(0, GW)], x_send.at[1])
-    wait(ob.at[:, :, 0, :, pl.ds(0, GW)], x_send.at[2])
-    wait(ob.at[:, :, 1, :, pl.ds(0, GW)], x_send.at[3])
-    for p, (_, _, rows) in enumerate(PIECES):
-        wait(po.at[p, pl.ds(0, 2 * rows)], y_send.at[p])
+    wait(po.at[pl.ds(0, 4)], y_send)
     wait(outv, out_sem)
+
+
+def copy_kernel(a, b, out_a, out_b, held, load_sem, store_sem):
+    parts = []
+    for i in range(2):
+        rows = pl.ds(i * (SEQ // 2), SEQ // 2)
+        for j, (src, dst) in enumerate(((a, out_a), (b, out_b))):
+            here = held.at[j, rows]
+            load = pltpu.make_async_copy(src.at[rows], here, load_sem.at[j, i])
+            load.start()
+            parts.append((load, pltpu.make_async_copy(here, dst.at[rows], store_sem)))
+    for load, store in parts:
+        load.wait()
+        store.start()
+    pltpu.make_async_copy(held, held, store_sem).wait()
 
 
 def per_device(
@@ -537,7 +550,7 @@
     anywhere = pl.BlockSpec(memory_space=pl.ANY)
     dma = pltpu.SemaphoreType.DMA
     shape = jax.ShapeDtypeStruct((SEQ, COLS), BF)
-    return pl.pallas_call(
+    results = pl.pallas_call(
         kernel,
         out_shape=(shape, shape),
         in_specs=[pl.BlockSpec(memory_space=pltpu.HBM)] * 11,
@@ -558,30 +571,31 @@
             pltpu.VMEM((2, 4, 2, 16, COLS), BF),
             pltpu.VMEM((2, SEQ, COLS), BF),
             pltpu.VMEM((2, SEQ, COLS), BF),
-            pltpu.VMEM((5, 256, COLS), BF),
-            pltpu.VMEM((5, 256, COLS), BF),
+            pltpu.VMEM((7, 256, COLS), BF),
+            pltpu.VMEM((7, 256, COLS), BF),
             dma((5,)),
+            dma((2,)),
+            dma,
+            dma,
+            dma,
+            dma((2,)),
+            dma,
+            dma((3,)),
+            dma,
+            dma((3,)),
+            dma,
             dma((4,)),
             dma,
-            dma,
+            dma((4,)),
+            dma,
+            dma((2,)),
             dma((3,)),
             dma((3,)),
-            dma((3,)),
-            dma((3,)),
-            dma((6,)),
-            dma((6,)),
-            dma((4,)),
-            dma((4,)),
-            dma((4,)),
-            dma((4,)),
-            dma((4,)),
-            dma((4,)),
-            dma((3,)),
-            dma((3,)),
-            dma((4,)),
-            dma((4, 20)),
-            dma((5,)),
-            dma((5,)),
+            dma,
+            dma((18,)),
+            dma((7,)),
+            dma,
+            dma((7,)),
         ],
         compiler_params=pltpu.CompilerParams(
             collective_id=0, has_side_effects=True, vmem_limit_bytes=56 * 2**20
@@ -599,6 +613,14 @@
         residual_tangent,
         jnp.asarray(CONST),
     )
+    return pl.pallas_call(
+        copy_kernel,
+        out_shape=(shape, shape),
+        in_specs=[anywhere, anywhere],
+        out_specs=(anywhere, anywhere),
+        scratch_shapes=[pltpu.VMEM((2, SEQ, COLS), BF), dma((2, 2)), dma],
+        compiler_params=pltpu.CompilerParams(vmem_limit_bytes=60 * 2**20),
+    )(*results)
 
 
 def solution(mesh):

time: 126 us -> 124 us (0.984)
  local copies, waits for them, and re-layouts: 3.65 us -> 0 us
    unnamed x4 -> x0, local copies, waits for them, and re-layouts: 3.65 us -> none
    pallas_call x0 -> x1, Pallas kernels: none -> 2.61 us  [per_device(): pl.pallas_call(copy_kernel, out_shape=(shape, shape), in_specs=[anywhere,...]
    pallas_call x1, Pallas kernels: 121 us -> 119 us  [per_device(): pl.pallas_call(kernel, out_shape=(shape, shape), in_specs=[pl.BlockSpec(m...]
where the time goes in v3:
time: 124 us; the launch traced here: 122 us
  Pallas kernels  121 us (98%)
    pallas_call x1, Pallas kernels, per_device(): pl.pallas_call(kernel, out_shape=(shape, shape), in_specs=[pl.BlockSpec(m...  119 us
    pallas_call x1, Pallas kernels, per_device(): pl.pallas_call(copy_kernel, out_shape=(shape, shape), in_specs=[anywhere,...  2.61 us

profile of v3, /device:TPU:10, one launch (start us, length us, event | category | flops | bytes accessed | tf_op | source)
XLA Modules:
  0.0 122.1 jit_solution(2015368782054057532)
XLA Ops:
  0.6 118.7 %shard_map.122 = (bf16[1024,640]{1,0:T(8,128)(2,1)}, bf16[1024,640]{1,0:T(8,128)(2,1)}) custom-call(bf16[3,128,3072]{2,1,0:T(8,128)(2,1)} %proj.1, bf16[3,128,3072]{2,1,0:T(8,128)(2,1)} %tan.1, s32[3,128]{1,0:T(4,128)} %bitcast.1, f32[2,3072]{1,0:T(2,128)} %gain_hbm.1, bf16[192,640]{1,0:T(8,128)(2,1)} %wout.1, s32[16]{0:T(128)} %time_hbm.1, f32[16]{0:T(128)} %ttan_hbm.1, ...), custom_call_target="tpu_custom_call" | custom-call | tf_op jit(solution)/shard_map/pallas_call | solution.py:553
  119.3 2.6 %shard_map.123 = (bf16[1024,640]{1,0:T(8,128)(2,1)}, bf16[1024,640]{1,0:T(8,128)(2,1)}) custom-call(bf16[1024,640]{1,0:T(8,128)(2,1)} %get-tuple-element.4.a, bf16[1024,640]{1,0:T(8,128)(2,1)} %get-tuple-element.5.b), custom_call_target="tpu_custom_call" | custom-call | tf_op jit(solution)/shard_map/pallas_call | solution.py:616

commit v4 on v3

--- a/solution.py
+++ b/solution.py
@@ -91,13 +91,11 @@
     wall,
     gall,
     resv,
-    outv,
     po,
     pr,
     small_sem,
     load_sem,
     res_sem,
-    out_sem,
     v_send,
     v_recv,
     q_send,
@@ -186,6 +184,13 @@
     mine = pl.ds(pl.multiple_of(head * ROWS, ROWS), ROWS)
     gate_cols = wgate.at[:, pl.ds(pl.multiple_of(head * COLS, 128), COLS)]
 
+    barrier = pltpu.get_barrier_semaphore()
+    for dy, dx in ORDER:
+        to = {"dp": dp, "head": lax.rem(y + dy, 2) * X + lax.rem(x + dx, X)}
+        pl.semaphore_signal(barrier, inc=1, device_id=to, device_id_type=MESH)
+    for to in (z_peer(1), z_peer(2), z_peer(3), other_core, y_chip(2), y_chip(3)):
+        pl.semaphore_signal(barrier, inc=1, device_id=to, device_id_type=MESH)
+
     for h in range(3):
 
         def load_v(g, _, h=h):
@@ -205,12 +210,6 @@
     local(res, resv.at[0], res_sem)
     local(rtan, resv.at[1], res_sem)
 
-    barrier = pltpu.get_barrier_semaphore()
-    for dy, dx in ORDER:
-        to = {"dp": dp, "head": lax.rem(y + dy, 2) * X + lax.rem(x + dx, X)}
-        pl.semaphore_signal(barrier, inc=1, device_id=to, device_id_type=MESH)
-    for to in (z_peer(1), z_peer(2), z_peer(3), other_core, y_chip(2), y_chip(3)):
-        pl.semaphore_signal(barrier, inc=1, device_id=to, device_id_type=MESH)
     pl.semaphore_wait(barrier, 13)
 
     wait(shard(0).at[z, c], wy_recv.at[0])
@@ -403,9 +402,10 @@
     src = shard(1).at[z, c]
     send(src, src, wy_send, wy_recv.at[2], y_chip(3))
     forward(0, 0, 0)
+    forward(1, 0, 0)
+    x_unit(2, 2, 0)
     swapped(0)
     x_unit(0, 0, 1)
-    forward(1, 0, 0)
     wait(shard(2).at[z, c], wy_recv.at[2])
     shard_along_z(2)
     forward(0, 1, 0)
@@ -417,7 +417,6 @@
     forward(1, 1, 0)
     x_unit(1, 1, 1)
     forward(0, 1, 1)
-    x_unit(2, 2, 0)
     forward(1, 0, 1)
     forward(1, 1, 1)
     swapped(2)
@@ -440,10 +439,8 @@
     wait(resv, res_sem)
 
     def finish(rows, attn, dattn):
-        outv[0, rows, :] = (resv[0, rows, :].astype(F32) + gate * attn).astype(BF)
-        outv[1, rows, :] = (resv[1, rows, :].astype(F32) + dgate * attn + gate * dattn).astype(BF)
-        local(outv.at[0, rows], out.at[rows], out_sem)
-        local(outv.at[1, rows], otan.at[rows], out_sem)
+        out[rows, :] = (resv[0, rows, :].astype(F32) + gate * attn).astype(BF)
+        otan[rows, :] = (resv[1, rows, :].astype(F32) + dgate * attn + gate * dattn).astype(BF)
 
     def project(rb, first, rows, yl):
         total = None
@@ -517,22 +514,18 @@
             pr[p, rows : 2 * rows].astype(F32),
         )
     wait(po.at[pl.ds(0, 4)], y_send)
-    wait(outv, out_sem)
-
-
-def copy_kernel(a, b, out_a, out_b, held, load_sem, store_sem):
-    parts = []
+
+
+def copy_kernel(a, b, out_a, out_b, sem):
+    copies = []
     for i in range(2):
         rows = pl.ds(i * (SEQ // 2), SEQ // 2)
         for j, (src, dst) in enumerate(((a, out_a), (b, out_b))):
-            here = held.at[j, rows]
-            load = pltpu.make_async_copy(src.at[rows], here, load_sem.at[j, i])
-            load.start()
-            parts.append((load, pltpu.make_async_copy(here, dst.at[rows], store_sem)))
-    for load, store in parts:
-        load.wait()
-        store.start()
-    pltpu.make_async_copy(held, held, store_sem).wait()
+            copies.append(pltpu.make_async_copy(src.at[rows], dst.at[rows], sem.at[j, i]))
+    for copy in copies:
+        copy.start()
+    for copy in copies:
+        copy.wait()
 
 
 def per_device(
@@ -552,9 +545,9 @@
     shape = jax.ShapeDtypeStruct((SEQ, COLS), BF)
     results = pl.pallas_call(
         kernel,
-        out_shape=(shape, shape),
+        out_shape=(pltpu.VMEM((SEQ, COLS), BF),) * 2,
         in_specs=[pl.BlockSpec(memory_space=pltpu.HBM)] * 11,
-        out_specs=(anywhere, anywhere),
+        out_specs=(pl.BlockSpec(memory_space=pltpu.VMEM),) * 2,
         scratch_shapes=[
             pltpu.VMEM((3, ROWS), jnp.int32),
             pltpu.VMEM((2, ATT_W), F32),
@@ -570,12 +563,10 @@
             pltpu.VMEM((2, 2, 4, 2, 192, COLS), BF),
             pltpu.VMEM((2, 4, 2, 16, COLS), BF),
             pltpu.VMEM((2, SEQ, COLS), BF),
-            pltpu.VMEM((2, SEQ, COLS), BF),
             pltpu.VMEM((7, 256, COLS), BF),
             pltpu.VMEM((7, 256, COLS), BF),
             dma((5,)),
             dma((2,)),
-            dma,
             dma,
             dma,
             dma((2,)),
@@ -618,8 +609,8 @@
         out_shape=(shape, shape),
         in_specs=[anywhere, anywhere],
         out_specs=(anywhere, anywhere),
-        scratch_shapes=[pltpu.VMEM((2, SEQ, COLS), BF), dma((2, 2)), dma],
-        compiler_params=pltpu.CompilerParams(vmem_limit_bytes=60 * 2**20),
+        scratch_shapes=[dma((2, 2))],
+        compiler_params=pltpu.CompilerParams(vmem_limit_bytes=8 * 2**20),
     )(*results)
 
 

time: 124 us -> 121 us (0.976)
  Pallas kernels: 121 us -> 118 us
    pallas_call x1, Pallas kernels: 119 us -> 117 us  [per_device(): pl.pallas_call(kernel, out_shape=(pltpu.VMEM((SEQ, COLS), BF),) * 2, in_s...]
where the time goes in v4:
time: 121 us; the launch traced here: 119 us
  Pallas kernels  118 us (98%)
    pallas_call x1, Pallas kernels, per_device(): pl.pallas_call(kernel, out_shape=(pltpu.VMEM((SEQ, COLS), BF),) * 2, in_s...  117 us

profile of v4, /device:TPU:10, one launch (start us, length us, event | category | flops | bytes accessed | tf_op | source)
XLA Modules:
  0.0 119.1 jit_solution(501548867535930364)
XLA Ops:
  0.6 116.8 %shard_map.122 = (bf16[1024,640]{1,0:T(8,128)(2,1)S(1)}, bf16[1024,640]{1,0:T(8,128)(2,1)S(1)}) custom-call(bf16[3,128,3072]{2,1,0:T(8,128)(2,1)} %proj.1, bf16[3,128,3072]{2,1,0:T(8,128)(2,1)} %tan.1, s32[3,128]{1,0:T(4,128)} %bitcast.1, f32[2,3072]{1,0:T(2,128)} %gain_hbm.1, bf16[192,640]{1,0:T(8,128)(2,1)} %wout.1, s32[16]{0:T(128)} %time_hbm.1, ...), custom_call_target="tpu_custom_call" | custom-call | tf_op jit(solution)/shard_map/pallas_call | solution.py:546
  117.5 1.5 %shard_map.123 = (bf16[1024,640]{1,0:T(8,128)(2,1)}, bf16[1024,640]{1,0:T(8,128)(2,1)}) custom-call(bf16[1024,640]{1,0:T(8,128)(2,1)S(1)} %get-tuple-element.4.a, bf16[1024,640]{1,0:T(8,128)(2,1)S(1)} %get-tuple-element.5.b), custom_call_target="tpu_custom_call" | custom-call | tf_op jit(solution)/shard_map/pallas_call | solution.py:607

commit v5 on v4

--- a/solution.py
+++ b/solution.py
@@ -32,6 +32,7 @@
     (3, 64, 32),
     (3, 96, 32),
 )
+ALL = 5
 PARTS = ((0, 256), (256, 128), (0, 384))
 
 ORDER = ((1, 0), (0, 1), (0, 3), (1, 2), (0, 2), (1, 1), (1, 3))
@@ -361,8 +362,17 @@
         src, k = unit(p, part, which, xr)
         send(src.at[1], src.at[1], x_send, f_recv.at[p], left)
 
+    def all_unit(p, which):
+        x_unit(p, 2, which)
+        src, _ = unit(p, 2, which, x)
+        send(src, src, x_send, f_recv.at[p], {"dp": dp, "head": y * X + lax.rem(x + 2, X)})
+
     def arrived(p):
         rb, first, rows = PIECES[p]
+        if p == ALL:
+            for which in (0, 1):
+                _, k = unit(p, 2, which, x)
+                wait(ob.at[rb, :, :, pl.ds(first, rows), pl.ds(0, GW)], x_recv.at[k])
         wait(ob.at[rb, :, :, pl.ds(first, rows), pl.ds(0, GW)], f_recv.at[p])
 
     wait(shard(3).at[z, c], wy_recv.at[3])
@@ -477,20 +487,17 @@
             own_block(0)
         elif p == 2:
             forward(3, 2, 1)
-            x_unit(5, 2, 0)
+            x_unit(6, 2, 0)
             forward(4, 2, 0)
-            x_unit(5, 2, 1)
+            x_unit(6, 2, 1)
+            forward(4, 2, 1)
+            all_unit(ALL, 0)
             own_block(1)
         elif p == 3:
-            forward(4, 2, 1)
-            x_unit(6, 2, 0)
-            forward(5, 2, 0)
-            x_unit(6, 2, 1)
-        elif p == 4:
-            forward(5, 2, 1)
+            all_unit(ALL, 1)
+            own_block(2)
             forward(6, 2, 0)
             forward(6, 2, 1)
-            own_block(2)
         elif p == 6:
             own_block(3)
 

time: 121 us -> 119 us (0.983)
    pallas_call x1, Pallas kernels: 117 us -> 115 us  [per_device(): pl.pallas_call(kernel, out_shape=(pltpu.VMEM((SEQ, COLS), BF),) * 2, in_s...]
where the time goes in v5:
time: 119 us; the launch traced here: 117 us
  Pallas kernels  117 us (98%)
    pallas_call x1, Pallas kernels, per_device(): pl.pallas_call(kernel, out_shape=(pltpu.VMEM((SEQ, COLS), BF),) * 2, in_s...  115 us

profile of v5, /device:TPU:10, one launch (start us, length us, event | category | flops | bytes accessed | tf_op | source)
XLA Modules:
  0.0 117.4 jit_solution(6372926243405621787)
XLA Ops:
  0.6 115.1 %shard_map.122 = (bf16[1024,640]{1,0:T(8,128)(2,1)S(1)}, bf16[1024,640]{1,0:T(8,128)(2,1)S(1)}) custom-call(bf16[3,128,3072]{2,1,0:T(8,128)(2,1)} %proj.1, bf16[3,128,3072]{2,1,0:T(8,128)(2,1)} %tan.1, s32[3,128]{1,0:T(4,128)} %bitcast.1, f32[2,3072]{1,0:T(2,128)} %gain_hbm.1, bf16[192,640]{1,0:T(8,128)(2,1)} %wout.1, s32[16]{0:T(128)} %time_hbm.1, ...), custom_call_target="tpu_custom_call" | custom-call | tf_op jit(solution)/shard_map/pallas_call | solution.py:553
  115.7 1.5 %shard_map.123 = (bf16[1024,640]{1,0:T(8,128)(2,1)}, bf16[1024,640]{1,0:T(8,128)(2,1)}) custom-call(bf16[1024,640]{1,0:T(8,128)(2,1)S(1)} %get-tuple-element.4.a, bf16[1024,640]{1,0:T(8,128)(2,1)S(1)} %get-tuple-element.5.b), custom_call_target="tpu_custom_call" | custom-call | tf_op jit(solution)/shard_map/pallas_call | solution.py:614

commit v6 on v5

--- a/solution.py
+++ b/solution.py
@@ -369,11 +369,13 @@
 
     def arrived(p):
         rb, first, rows = PIECES[p]
-        if p == ALL:
-            for which in (0, 1):
-                _, k = unit(p, 2, which, x)
-                wait(ob.at[rb, :, :, pl.ds(first, rows), pl.ds(0, GW)], x_recv.at[k])
         wait(ob.at[rb, :, :, pl.ds(first, rows), pl.ds(0, GW)], f_recv.at[p])
+
+    def arrived_near(p):
+        rb, first, rows = PIECES[p]
+        for which in (0, 1):
+            _, k = unit(p, 2, which, x)
+            wait(ob.at[rb, :, :, pl.ds(first, rows), pl.ds(0, GW)], x_recv.at[k])
 
     wait(shard(3).at[z, c], wy_recv.at[3])
     shard_along_z(3)
@@ -463,14 +465,36 @@
             total = term if total is None else total + term
         return total
 
+    def project_from(rb, first, rows, yl, offsets):
+        total = None
+        for gy in (0, 1):
+            for offset in offsets:
+                at = lax.rem(x + offset, X)
+                col = pl.ds(pl.multiple_of(at * GW, 128), GW)
+                term = jnp.dot(
+                    ob[rb, gy, :, first : first + rows, col].reshape(2 * rows, GW),
+                    wall[yl, gy, at].reshape(GW, COLS),
+                    preferred_element_type=F32,
+                )
+                total = term if total is None else total + term
+        return total
+
     def own_block(rb):
         total = project(rb, 0, ROWS, y)
         start = pl.multiple_of(y * HALF + rb * ROWS, ROWS)
         finish(pl.ds(start, ROWS), total[:ROWS], total[ROWS:])
 
     for p, (rb, first, rows) in enumerate(PIECES):
+        if p == ALL:
+            arrived_near(p)
+            near = project_from(rb, first, 2 * rows, 1 - y, (0, 1, 3))
         arrived(p)
-        total = project(rb, first, rows, 1 - y)
+        if p < ALL:
+            total = project(rb, first, rows, 1 - y)
+        else:
+            at = (p - ALL) * rows
+            total = jnp.concatenate([near[at : at + rows], near[2 * rows + at : 3 * rows + at]])
+            total = total + project_from(rb, first, rows, 1 - y, (2,))
         both = pl.ds(0, 2 * rows)
         po[p, both] = total.astype(BF)
         send(po.at[p, both], pr.at[p, both], y_send, y_recv.at[p], partner)
@@ -492,9 +516,9 @@
             x_unit(6, 2, 1)
             forward(4, 2, 1)
             all_unit(ALL, 0)
+            all_unit(ALL, 1)
             own_block(1)
         elif p == 3:
-            all_unit(ALL, 1)
             own_block(2)
             forward(6, 2, 0)
             forward(6, 2, 1)
@@ -525,8 +549,8 @@
 
 def copy_kernel(a, b, out_a, out_b, sem):
     copies = []
-    for i in range(2):
-        rows = pl.ds(i * (SEQ // 2), SEQ // 2)
+    for i in range(1):
+        rows = pl.ds(i * (SEQ // 1), SEQ // 1)
         for j, (src, dst) in enumerate(((a, out_a), (b, out_b))):
             copies.append(pltpu.make_async_copy(src.at[rows], dst.at[rows], sem.at[j, i]))
     for copy in copies:
@@ -616,7 +640,7 @@
         out_shape=(shape, shape),
         in_specs=[anywhere, anywhere],
         out_specs=(anywhere, anywhere),
-        scratch_shapes=[dma((2, 2))],
+        scratch_shapes=[dma((2, 1))],
         compiler_params=pltpu.CompilerParams(vmem_limit_bytes=8 * 2**20),
     )(*results)
 

time: 119 us -> 119 us (level)
  no operation moved by 1% of the time
where the time goes in v6:
time: 119 us; the launch traced here: 117 us
  Pallas kernels  116 us (97%)
    pallas_call x1, Pallas kernels, per_device(): pl.pallas_call(kernel, out_shape=(pltpu.VMEM((SEQ, COLS), BF),) * 2, in_s...  115 us

profile of v6, /device:TPU:10, one launch (start us, length us, event | category | flops | bytes accessed | tf_op | source)
XLA Modules:
  0.0 116.9 jit_solution(8234603926230108282)
XLA Ops:
  0.6 114.6 %shard_map.122 = (bf16[1024,640]{1,0:T(8,128)(2,1)S(1)}, bf16[1024,640]{1,0:T(8,128)(2,1)S(1)}) custom-call(bf16[3,128,3072]{2,1,0:T(8,128)(2,1)} %proj.1, bf16[3,128,3072]{2,1,0:T(8,128)(2,1)} %tan.1, s32[3,128]{1,0:T(4,128)} %bitcast.1, f32[2,3072]{1,0:T(2,128)} %gain_hbm.1, bf16[192,640]{1,0:T(8,128)(2,1)} %wout.1, s32[16]{0:T(128)} %time_hbm.1, ...), custom_call_target="tpu_custom_call" | custom-call | tf_op jit(solution)/shard_map/pallas_call | solution.py:577
  115.3 1.5 %shard_map.123 = (bf16[1024,640]{1,0:T(8,128)(2,1)}, bf16[1024,640]{1,0:T(8,128)(2,1)}) custom-call(bf16[1024,640]{1,0:T(8,128)(2,1)S(1)} %get-tuple-element.4.a, bf16[1024,640]{1,0:T(8,128)(2,1)S(1)} %get-tuple-element.5.b), custom_call_target="tpu_custom_call" | custom-call | tf_op jit(solution)/shard_map/pallas_call | solution.py:638

commit v7 on v6

--- a/solution.py
+++ b/solution.py
@@ -213,13 +213,13 @@
 
     pl.semaphore_wait(barrier, 13)
 
+    wait(sv, load_sem.at[0])
+    sends_v(0)
+    sends_v(1)
     wait(shard(0).at[z, c], wy_recv.at[0])
     src = shard(0).at[z, c]
     send(src, src, wy_send, wy_recv.at[3], y_chip(3))
     shard_along_z(0)
-    wait(sv, load_sem.at[0])
-    sends_v(0)
-    sends_v(1)
     send(gate_cols, gall.at[yh, z, c], g_send.at[0], g_recv.at[0], y_chip(2))
 
     for i, (_, dst) in enumerate(small):
@@ -548,11 +548,10 @@
 
 
 def copy_kernel(a, b, out_a, out_b, sem):
-    copies = []
-    for i in range(1):
-        rows = pl.ds(i * (SEQ // 1), SEQ // 1)
-        for j, (src, dst) in enumerate(((a, out_a), (b, out_b))):
-            copies.append(pltpu.make_async_copy(src.at[rows], dst.at[rows], sem.at[j, i]))
+    copies = (
+        pltpu.make_async_copy(a, out_a, sem.at[0]),
+        pltpu.make_async_copy(b, out_b, sem.at[1]),
+    )
     for copy in copies:
         copy.start()
     for copy in copies:
@@ -640,7 +639,7 @@
         out_shape=(shape, shape),
         in_specs=[anywhere, anywhere],
         out_specs=(anywhere, anywhere),
-        scratch_shapes=[dma((2, 1))],
+        scratch_shapes=[dma((2,))],
         compiler_params=pltpu.CompilerParams(vmem_limit_bytes=8 * 2**20),
     )(*results)
 

time: 119 us -> 118 us (level)
  no operation moved by 1% of the time
where the time goes in v7:
time: 118 us; the launch traced here: 117 us
  Pallas kernels  116 us (98%)
    pallas_call x1, Pallas kernels, per_device(): pl.pallas_call(kernel, out_shape=(pltpu.VMEM((SEQ, COLS), BF),) * 2, in_s...  115 us

profile of v7, /device:TPU:10, one launch (start us, length us, event | category | flops | bytes accessed | tf_op | source)
XLA Modules:
  0.0 117.1 jit_solution(15336118039945638939)
XLA Ops:
  0.6 114.8 %shard_map.122 = (bf16[1024,640]{1,0:T(8,128)(2,1)S(1)}, bf16[1024,640]{1,0:T(8,128)(2,1)S(1)}) custom-call(bf16[3,128,3072]{2,1,0:T(8,128)(2,1)} %proj.1, bf16[3,128,3072]{2,1,0:T(8,128)(2,1)} %tan.1, s32[3,128]{1,0:T(4,128)} %bitcast.1, f32[2,3072]{1,0:T(2,128)} %gain_hbm.1, bf16[192,640]{1,0:T(8,128)(2,1)} %wout.1, s32[16]{0:T(128)} %time_hbm.1, ...), custom_call_target="tpu_custom_call" | custom-call | tf_op jit(solution)/shard_map/pallas_call | solution.py:576
  115.4 1.5 %shard_map.123 = (bf16[1024,640]{1,0:T(8,128)(2,1)}, bf16[1024,640]{1,0:T(8,128)(2,1)}) custom-call(bf16[1024,640]{1,0:T(8,128)(2,1)S(1)} %get-tuple-element.4.a, bf16[1024,640]{1,0:T(8,128)(2,1)S(1)} %get-tuple-element.5.b), custom_call_target="tpu_custom_call" | custom-call | tf_op jit(solution)/shard_map/pallas_call | solution.py:637
